TPU v7x, 256 devices: a whole 4x4x8 slice. The times are simulated.
256 devices in a mesh: group: 8 (over y, core), page: 32 (over x, z).
Axes of the slice: x: 4, y: 4, z: 8, core: 2. Of those that a mesh axis runs over, the one named last changes fastest.
Arguments:
- queries: bfloat16 [8, 2, 128, 576], P('group', None, 'page'), may hold values from -260 to 260
- cache: bfloat16 [8, 3072, 64, 576], P('group', 'page'), may hold values from -18 to 18
- slot_page: int32 [8, 3072], P('group', 'page'), may hold values from 0 to 3071, as said below
- lengths: int32 [8], P('group'), may hold values from 24576 to 196608, as said below
- w_uv: bfloat16 [128, 512, 128], P('page'), may hold values from -0.25 to 0.25
- w_out: bfloat16 [16384, 7168], P('page', 'group'), may hold values from -0.09375 to 0.09375
Outputs:
- output: bfloat16 [8, 2, 7168], P(None, None, ('group', 'page'))
Inputs may be any that keep to these rules, and one draw needn't show every extreme that they name: `slot_page`: each request's row is a permutation; each index of page holds 96 consecutive logical pages. `lengths`: one request has exactly 196608 tokens.
All inputs are finite; a program needn't handle non-finite values.
Results may differ from a plain program's by a relative error of at most 0.015.
Values may be sent and summed in bfloat16 or wider, within the bound.
A program may use at most 64 MiB of HBM per device.

v0:
```python
import jax
import jax.numpy as jnp
from jax import lax
from jax.sharding import PartitionSpec as P

score_scale = 192.0 ** (-0.5)
masked_fill = -1e30


def combined_all(shard, axis, combine):
    everything = jax.tree.map(lambda part: lax.all_gather(part, axis), shard)
    initial = jax.tree.map(lambda part: part[0], everything)

    def hop(k, so_far):
        return combine(so_far, jax.tree.map(lambda part: part[k], everything))

    return lax.fori_loop(1, lax.axis_size(axis), hop, initial)


def join_partials(left_part, right_part):
    peak_value = jnp.maximum(left_part[0], right_part[0])
    left_factor = jnp.exp(left_part[0] - peak_value)
    right_factor = jnp.exp(right_part[0] - peak_value)
    joined_total = left_part[1] * left_factor + right_part[1] * right_factor
    joined_numer = left_part[2] * left_factor[:, None] + right_part[2] * right_factor[:, None]
    return (peak_value, joined_total, joined_numer)


def body(queries, cache, slot_page, lengths, w_uv, w_out):
    whole_query = lax.all_gather(queries, "page", axis=2, tiled=True)
    new_tokens = whole_query.shape[1]
    heads = whole_query.shape[2]
    width = whole_query.shape[3]
    latent = w_uv.shape[1]
    page_rows = cache.shape[2]
    heads_dev = w_uv.shape[0]
    key_rows = cache.reshape(-1, width)
    positions = (
        slot_page[0][:, None] * page_rows + jnp.arange(page_rows, dtype=jnp.int32)[None, :]
    ).reshape(-1)
    limits = lengths[0] - new_tokens + jnp.arange(new_tokens, dtype=jnp.int32)
    live_mask = positions[None, :] <= limits[:, None]
    live_mask = jnp.broadcast_to(
        live_mask[:, None, :], (new_tokens, heads, positions.shape[0])
    ).reshape(new_tokens * heads, -1)
    scores = (
        lax.dot_general(
            whole_query.reshape(-1, width),
            key_rows,
            (((1,), (1,)), ((), ())),
            preferred_element_type=jnp.float32,
        )
        * score_scale
    )
    masked = jnp.where(live_mask, scores, masked_fill)
    local_max = jnp.max(masked, axis=1)
    weights = jnp.where(live_mask, jnp.exp(masked - local_max[:, None]), 0.0).astype(jnp.bfloat16)
    local_sum = jnp.sum(weights.astype(jnp.float32), axis=1)
    numerator = jnp.dot(weights, key_rows[:, :latent], preferred_element_type=jnp.float32)
    merged = combined_all((local_max, local_sum, numerator), "page", join_partials)
    start = lax.axis_index("page") * heads_dev
    numer_all = merged[2].reshape(new_tokens, heads, latent)
    total_all = merged[1].reshape(new_tokens, heads)
    numer_own = lax.dynamic_slice_in_dim(numer_all, start, heads_dev, 1)
    total_own = lax.dynamic_slice_in_dim(total_all, start, heads_dev, 1)
    attended = (numer_own / total_own[:, :, None]).astype(jnp.bfloat16)
    values = jnp.einsum("thl,hlv->thv", attended, w_uv, preferred_element_type=jnp.float32).astype(
        jnp.bfloat16
    )
    flat_values = values.reshape(1, new_tokens, -1)
    every_request = lax.all_gather(flat_values, "group", axis=0, tiled=True)
    requests = every_request.shape[0]
    terms = jnp.dot(
        every_request.reshape(requests * new_tokens, -1), w_out, preferred_element_type=jnp.float32
    )
    terms = terms.reshape(requests, new_tokens, -1)
    summed = lax.psum_scatter(terms, "page", scatter_dimension=2, tiled=True)
    return summed.astype(jnp.bfloat16)


def solution(mesh):
    in_specs = (
        P("group", None, "page", None),
        P("group", "page", None, None),
        P("group", "page"),
        P("group"),
        P("page", None, None),
        P("page", "group"),
    )
    out_specs = P(None, None, ("group", "page"))
    return jax.shard_map(body, mesh=mesh, in_specs=in_specs, out_specs=out_specs, check_vma=False)
```

profile of v0, /device:TPU:8, one launch (start us, length us, event | category | flops | bytes accessed | tf_op | source)
XLA Modules:
  0.0 411.4 jit_solution(5593750431255995264)
XLA Ops:
  8.8 52.5 %all_gather.24 = bf16[1,2,128,576]{3,1,0,2:T(2,128)(2,1)S(1)} all-gather(bf16[1,2,4,576]{3,1,0,2:T(2,128)(2,1)S(1)} %copy.18), channel_id=1, replica_groups=mesh['group'=8,'page'=32] {'page'}, dimensions={2}, use_global_device_ids=true | all-gather | bytes 304128 | tf_op jit(solution)/shard_map/all_gather | solution.py:30
  62.5 6.2 %fusion.14 = (f32[256]{0:T(256)S(1)}, f32[256,6144]{1,0:T(8,128)S(1)}) fusion(bf16[6144,576]{1,0:T(8,128)(2,1)} %bitcast.60, bf16[72,8,2,128]{3,2,1,0:T(2,128)(2,1)S(1)} %bitcast.64, pred[2,6144]{1,0:T(4,128)(4,1)S(1)} %broadcast_compare_fusion), kind=kOutput, calls=%fused_computation.33 | convolution fusion | flops 1816657664 | bytes 13677568 | tf_op jit(solution)/shard_map/dot_general | solution.py:47
  68.7 1.7 convert_reduce_fusion
  70.4 2.7 fusion.2
  73.1 42.0 %all-gather.4 = f32[32,1,256]{2,1,0:T(1,128)S(1)} all-gather(f32[1,1,256]{2,1,0:T(1,128)S(1)} %bitcast.74), channel_id=3, replica_groups=mesh['group'=8,'page'=32] {'page'}, dimensions={0}, use_global_device_ids=true | all-gather | bytes 33792 | tf_op jit(solution)/shard_map/all_gather | solution.py:11
  115.1 40.7 %all-gather.3 = f32[32,1,256]{2,1,0:T(1,128)S(1)} all-gather(f32[1,1,256]{2,1,0:T(1,128)S(1)} %bitcast.73), channel_id=2, replica_groups=mesh['group'=8,'page'=32] {'page'}, dimensions={0}, use_global_device_ids=true | all-gather | bytes 33792 | tf_op jit(solution)/shard_map/all_gather | solution.py:11
  157.1 54.4 %all-gather.7.cloned.1.call-done = f32[8192,512]{1,0:T(8,128)} async-done(((f32[256,512]{1,0:T(8,128)}), f32[8192,512]{1,0:T(8,128)}) %all-gather.7.cloned.1.call-update) | async-done | bytes 16777232 | tf_op jit(solution)/shard_map/all_gather | solution.py:11
  212.6 39.7 %while.19 = (s32[]{:T(128)}, f32[256]{0:T(256)S(1)}, f32[256]{0:T(256)S(1)}, f32[256,512]{1,0:T(8,128)S(1)}, f32[32,256]{1,0:T(8,128)S(1)}, /*index=5*/f32[32,25...) while((s32[]{:T(128)}, f32[256]{0:T(256)S(1)}, f32[256]{0:T(256)S(1)}, ...), condition=%wide.region_3.4_spmd, body=%wide.region_2.3_spmd.sunk | while | flops 394757 | bytes 1587351 | solution.py:17
  212.7 1.2 fusion.19
  213.9 1.2 fusion.19
  215.2 1.2 fusion.19
  216.5 1.2 fusion.19
  217.8 1.2 fusion.19
  219.1 1.2 fusion.19
  220.3 1.2 fusion.19
  221.6 1.2 fusion.19
  222.9 1.2 fusion.19
  224.2 1.2 fusion.19
  225.5 1.2 fusion.19
  226.7 1.2 fusion.19
  228.0 1.2 fusion.19
  229.3 1.2 fusion.19
  252.7 11.6 %all_gather.31 = bf16[8,2,512]{2,1,0:T(2,128)(2,1)S(1)} all-gather(bf16[1,2,512]{2,1,0:T(2,128)(2,1)S(1)} %fusion.4), channel_id=1, replica_groups=mesh['group'=8,'page'=32] {'group'}, dimensions={0}, use_global_device_ids=true | all-gather | bytes 18432 | tf_op jit(solution)/shard_map/all_gather | solution.py:71
  264.6 139.3 %all-reduce = bf16[8,2,896]{2,0,1:T(8,128)(2,1)S(1)} all-reduce(f32[8,2,896]{2,0,1:T(8,128)S(1)} %fusion.5), channel_id=5, replica_groups=mesh['group'=8,'page'=32] {'page'}, use_global_device_ids=true, to_apply=%region_4.5.clone | all-reduce | flops 14336 | bytes 86016
  (112 shorter events, 27.4 us)
Async XLA Ops:
  6.5 257.8 %copy-start = (bf16[512,896]{1,0:T(8,128)(2,1)S(1)}, bf16[512,896]{1,0:T(8,128)(2,1)}, u32[]{:S(2)}) copy-start(bf16[512,896]{1,0:T(8,128)(2,1)} %param.13) | copy-start | bytes 2752516
  6.5 205.0 %all-gather.7.cloned.1.call-start = ((), (), s32[]{:S(2)}) async-start(), calls=%async_computation | async-start | bytes 17301504 | tf_op jit(solution)/shard_map/all_gather | solution.py:11
  62.4 7.9 %slice-start = ((s8[7864320]{0:T(1024)(128)(4,1)}), s8[4194304]{0:T(1024)(128)(4,1)S(1)}, s32[]{:S(2)}) async-start(s8[7864320]{0:T(1024)(128)(4,1)} %bitcast.61), calls=%async_computation.1 | async-start | bytes 8388608
  62.4 7.9 %slice-start.1 = ((s8[7864320]{0:T(1024)(128)(4,1)}), s8[3670016]{0:T(1024)(128)(4,1)S(1)}, s32[]{:S(2)}) async-start(s8[7864320]{0:T(1024)(128)(4,1)} %bitcast.61), calls=%async_computation.2 | async-start | bytes 7340032
  70.4 85.4 %copy-start.2 = (u32[256]{0:T(256)S(1)}, u32[256]{0:T(256)}, u32[]{:S(2)}) copy-start(u32[256]{0:T(256)} %constant.67) | copy-start | bytes 3076
  73.1 179.4 %copy-start.1 = (bf16[4,512,128]{2,1,0:T(8,128)(2,1)S(1)}, bf16[4,512,128]{2,1,0:T(8,128)(2,1)}, u32[]{:S(2)}) copy-start(bf16[4,512,128]{2,1,0:T(8,128)(2,1)} %param.12) | copy-start | bytes 1572868
Sparse Core Ops, SparseCore 0:
  73.2 138.2 all-gather.6
where the time goes:
time: 413 us; the launch traced here: 411 us
  blocking collectives  286 us (69%)
  waiting for transfers between devices  54.4 us (13%)
  other arithmetic  40.8 us (10%)
  between operations  14.9 us (4%)
  matrix products  9.34 us (2%)
  local copies, waits for them, and re-layouts  4.74 us (1%)
    unnamed x1, blocking collectives  139 us
    all_gather x2, blocking collectives, combined_all(): everything = jax.tree.map(lambda part: lax.all_gather(part, axis), shard)  82.7 us
    all_gather x1, waiting for transfers between devices, combined_all(): everything = jax.tree.map(lambda part: lax.all_gather(part, axis), shard)  54.4 us
    all_gather x1, blocking collectives, body(): whole_query = lax.all_gather(queries, 'page', axis=2, tiled=True)  52.5 us
    add x31, other arithmetic, join_partials(): left_part[2] * left_factor[:, None] + right_part[2] * right_factor[:, None]  37.6 us
    all_gather x1, blocking collectives, body(): every_request = lax.all_gather(flat_values, 'group', axis=0, tiled=True)  11.6 us
  transfers between devices with their start and end apart: 1, of which 1 were waited for; matrix products, arithmetic and copies ran while one was open for 0% of the time, Pallas kernels for 0%

commit v1 on v0

v1 whole, which is shorter than its diff:
```python
import functools

import jax
import jax.numpy as jnp
from jax import lax
from jax.experimental import pallas as pl
from jax.experimental.pallas import tpu as pltpu
from jax.sharding import PartitionSpec as P

MESH = pl.DeviceIdType.MESH
F32 = jnp.float32
BF16 = jnp.bfloat16
score_scale = 192.0 ** (-0.5)
log2_e = 1.4426950408889634
masked_fill = -1e30
out_group = 32
step_keys = 1024
tile_keys = 256


def dot(a, b, contract_b=0):
    return lax.dot_general(a, b, (((1,), (contract_b,)), ((), ())), preferred_element_type=F32)


def kernel(
    sizes,
    q_hbm,
    k_hbm,
    page_hbm,
    length_hbm,
    up_hbm,
    out_hbm,
    result,
    q_in,
    q_rows,
    q_packed,
    q_all,
    keys,
    pages,
    length,
    w_up,
    w_out,
    w_placed,
    bias,
    scores,
    probs,
    peaks,
    sums,
    numer,
    num_send,
    num_recv,
    stat_send,
    stat_recv,
    low_stat_send,
    low_stat_recv,
    low_send,
    low_recv,
    head_values,
    term_send,
    term_recv,
    last_send,
    last_recv,
    local_sem,
    key_sem,
    qz_send,
    qz_recv,
    qx_send,
    qx_recv,
    st_send,
    st_recv,
    nx_send,
    nx_recv,
    ls_send,
    ls_recv,
    nz_send,
    nz_recv,
    v_send,
    v_recv,
    tx_send,
    tx_recv,
    tz_send,
    tz_recv,
):
    NX, NZ, NG, own_columns = sizes
    width = q_in.shape[-1]
    latent = w_up.shape[1]
    half = latent // 2
    key_rows = keys.shape[0]
    rows = q_all.shape[0]
    block = rows // NX
    steps = key_rows // step_keys
    tokens, heads = q_in.shape[1], q_in.shape[2]

    g = lax.axis_index("group")
    page = lax.axis_index("page")
    x, z = lax.div(page, NZ), lax.rem(page, NZ)

    def along_x(k):
        return {"page": lax.rem(x + k + NX, NX) * NZ + z}

    def along_z(k):
        return {"page": x * NZ + lax.rem(z + k + NZ, NZ)}

    def along_g(k):
        return {"group": lax.rem(g + k + NG, NG)}

    def send(source, target, send_sem, recv_sem, device):
        copy = pltpu.make_async_remote_copy(
            src_ref=source,
            dst_ref=target,
            send_sem=send_sem,
            recv_sem=recv_sem,
            device_id=device,
            device_id_type=MESH,
        )
        copy.start()
        return copy

    sent = []
    far_z = sorted(range(1, NZ), key=lambda k: -min(k, NZ - k))
    far_x = sorted(range(1, NX), key=lambda k: -min(k, NX - k))

    barrier = pltpu.get_barrier_semaphore()
    for k in range(1, NX):
        pl.semaphore_signal(barrier, inc=1, device_id=along_x(k), device_id_type=MESH)
    for k in range(1, NZ):
        pl.semaphore_signal(barrier, inc=1, device_id=along_z(k), device_id_type=MESH)
    for k in range(1, NG):
        pl.semaphore_signal(barrier, inc=1, device_id=along_g(k), device_id_type=MESH)

    def local(source, target, sem):
        copy = pltpu.make_async_copy(source, target, sem)
        copy.start()
        return copy

    q_copy = local(q_hbm, q_in, local_sem.at[0])
    page_copy = local(page_hbm, pages, local_sem.at[1])
    length_copy = local(length_hbm, length, local_sem.at[2])
    out_copy = local(out_hbm, w_out, local_sem.at[3])
    key_copies = [
        local(
            k_hbm.at[pl.ds(c * step_keys, step_keys)],
            keys.at[pl.ds(c * step_keys, step_keys)],
            key_sem.at[c],
        )
        for c in range(steps)
    ]
    up_copy = local(up_hbm, w_up, local_sem.at[4])

    q_copy.wait()
    q_rows[:, 512:768] = jnp.zeros((8, 256), F32)
    for t in range(tokens):
        q_rows[t * heads : (t + 1) * heads, 0:width] = q_in[0, t].astype(F32)
    q_packed[0, :, 0:128] = jnp.concatenate(
        [q_rows[:, 0:128], q_rows[:, 128:256]], axis=0
    ).astype(BF16)
    q_packed[0, :, 128:384] = jnp.concatenate(
        [q_rows[:, 256:512], q_rows[:, 512:768]], axis=0
    ).astype(BF16)
    pl.semaphore_wait(barrier, NX + NZ + NG - 3)
    parts = ((0, 128), (128, 384))
    places = ((0, 256), (256, 640))
    q_z = [{}, {}]
    for c, (low, high) in enumerate(parts):
        for k in far_z:
            q_z[c][k] = send(
                q_packed.at[0, :, low:high],
                q_packed.at[k, :, low:high],
                qz_send.at[c, k],
                qz_recv.at[c, k],
                along_z(k),
            )

    page_copy.wait()
    length_copy.wait()
    lane = lax.broadcasted_iota(jnp.int32, (8, 128), 1)
    token = lax.broadcasted_iota(jnp.int32, (8, 128), 0) // heads
    limit = length[0] - tokens + token
    for i in range(key_rows // 128):
        held = jnp.where(lane < 64, pages[0, 2 * i], pages[0, 2 * i + 1])
        position = held * 64 + lax.rem(lane, 64)
        bias[:, i * 128 : (i + 1) * 128] = jnp.where(position <= limit, 0.0, masked_fill)
    x_columns = own_columns * NZ
    x_lanes = out_group * NZ

    def place_columns():
        out_copy.wait()
        place = lax.broadcasted_iota(jnp.int32, (1, x_lanes), 1)
        inside = lax.rem(place, out_group)
        wanted = lax.div(place, out_group) * own_columns + inside
        wanted = jnp.where(inside < own_columns, wanted, -(2**20))
        for i in range(NX):
            low = i * x_columns // 128 * 128
            high = min(-(-(i + 1) * x_columns // 128) * 128, w_out.shape[1])
            column = lax.broadcasted_iota(jnp.int32, (high - low, x_lanes), 0)
            pick = jnp.where(column == wanted + (i * x_columns - low), 1.0, 0.0).astype(BF16)
            w_placed[:, i * x_lanes : (i + 1) * x_lanes] = dot(w_out[:, low:high], pick).astype(BF16)

    q_x = [{}, {}]
    relayed = [{}, {}]

    def q_block(c, first, target, count, k, sem):
        low, high = places[c]
        return send(
            q_all.at[pl.ds(first, count), low:high],
            q_all.at[pl.ds(target, count), low:high],
            qx_send.at[c, sem],
            qx_recv.at[c, sem],
            along_x(k),
        )

    for c in range(2):
        for k in far_z[::-1]:
            q_z[c][k].wait_recv()
        for k in range(0, NZ, 2):
            pair = []
            for j in (k, k + 1):
                part = q_packed[j, :, parts[c][0] : parts[c][1]].astype(F32)
                pair.append(
                    jnp.concatenate([part[0:8], part[8:16, 0:128]], axis=1)
                )
            q_all[k * 8 : k * 8 + 16, places[c][0] : places[c][1]] = jnp.concatenate(
                pair, axis=0
            ).astype(BF16)
        for k in far_x:
            if NX != 4 or k != 2:
                q_x[c][k] = q_block(c, 0, k * block, block, k, k)
        if c == 0:
            place_columns()
    if NX == 4:
        part = block // 2
        for c in range(2):
            q_x[c][1].wait_recv()
            relayed[c][1] = q_block(c, block, 2 * block, part, 1, 0)
            q_x[c][3].wait_recv()
            relayed[c][3] = q_block(c, 3 * block + part, 2 * block + part, part, -1, 2)
    for copy in key_copies:
        copy.wait()

    def wait_queries(c):
        for copy in (relayed[c] if NX == 4 else q_x[c]).values():
            copy.wait_recv()

    wait_queries(0)

    @pl.loop(0, steps)
    def _(c):
        for n in range(step_keys // tile_keys):
            at = pl.ds(pl.multiple_of(c * step_keys + n * tile_keys, tile_keys), tile_keys)
            scores[:, at] = dot(q_all[:, 0:256], keys[at, 0:256], 1)

    wait_queries(1)
    peaks[...] = jnp.full(peaks.shape, masked_fill, F32)

    @pl.loop(0, steps)
    def _(c):
        largest = peaks[...]
        for n in range(step_keys // tile_keys):
            at = pl.ds(pl.multiple_of(c * step_keys + n * tile_keys, tile_keys), tile_keys)
            s = scores[:, at] + dot(q_all[:, 256:width], keys[at, 256:width], 1)
            s = (s * (score_scale * log2_e)).reshape(rows // 8, 8, tile_keys) + bias[:, at][None]
            s = s.reshape(rows, tile_keys)
            scores[:, at] = s
            for j in range(0, tile_keys, 128):
                largest = jnp.maximum(largest, s[:, j : j + 128])
        peaks[...] = largest

    top = jnp.max(peaks[...], axis=1, keepdims=True)
    peaks[...] = jnp.broadcast_to(top, peaks.shape)
    sums[...] = jnp.zeros(sums.shape, F32)
    numer[...] = jnp.zeros(numer.shape, F32)

    @pl.loop(0, steps)
    def _(c):
        total = sums[...]
        top_here = peaks[...]
        pieces = []
        for n in range(step_keys // 128):
            at = pl.ds(pl.multiple_of(c * step_keys + n * 128, 128), 128)
            p = jnp.exp2(scores[:, at] - top_here)
            total = total + p
            p = p.astype(BF16)
            probs[:, at] = p
            pieces.append(p)
        sums[...] = total
        here = pl.ds(pl.multiple_of(c * step_keys, step_keys), step_keys)
        numer[0] += dot(jnp.concatenate(pieces, axis=1), keys[here, 0:half])

    total = jnp.broadcast_to(jnp.sum(sums[...], axis=1, keepdims=True), (rows, 128))
    sums[...] = total
    owner = lax.div(lax.broadcasted_iota(jnp.int32, (8, 128), 1), 8)
    for i in range(NX):
        tile = jnp.zeros((8, 128), F32)
        for v in range(NZ):
            at = pl.ds(i * block + v * 8, 8)
            tile = jnp.where(owner == v, peaks[at, :], tile)
            tile = jnp.where(owner == v + 8, sums[at, :], tile)
        stat_send[i] = tile
    stats = {}
    for k in far_x:
        stats[k] = send(
            stat_send.at[k], stat_recv.at[k], st_send.at[k], st_recv.at[k], along_x(-k)
        )

    num_x = [{}, {}]

    def send_half(h):
        num_send[h] = numer[h].astype(BF16)
        for k in far_x:
            num_x[h][k] = send(
                num_send.at[h, pl.ds(k * block, block)],
                num_recv.at[h, k],
                nx_send.at[h, k],
                nx_recv.at[h, k],
                along_x(-k),
            )

    send_half(0)

    @pl.loop(0, steps)
    def _(c):
        here = pl.ds(pl.multiple_of(c * step_keys, step_keys), step_keys)
        numer[1] += dot(probs[:, here], keys[here, half:latent])

    send_half(1)

    for k in far_x[::-1]:
        stats[k].wait_recv()
    found = [stat_send[0]] + [stat_recv[k] for k in range(1, NX)]
    factors = [[] for _ in found]
    for v in range(NZ):
        tops = [jnp.broadcast_to(f[:, 8 * v : 8 * v + 1], (8, 128)) for f in found]
        top_x = functools.reduce(jnp.maximum, tops)
        total_x = jnp.zeros((8, 128), F32)
        for f, t, held in zip(found, tops, factors):
            held.append(jnp.exp2(t - top_x))
            total_x = total_x + f[:, 64 + 8 * v : 64 + 8 * v + 1] * held[v]
        low_stat_send[v] = jnp.where(lane < 64, top_x, total_x)
    factors = [
        jnp.concatenate([jnp.concatenate(held, axis=0)] * (half // 128), axis=1) for held in factors
    ]
    low_stats = {}
    for k in far_z:
        low_stats[k] = send(
            low_stat_send.at[k],
            low_stat_recv.at[k],
            ls_send.at[k],
            ls_recv.at[k],
            along_z(-k),
        )

    num_z = [{}, {}]
    own_half = []
    for h in range(2):
        for k in far_x[::-1]:
            num_x[h][k].wait_recv()
        merged = numer[h, 0:block, :] * factors[0]
        for k in range(1, NX):
            merged = merged + num_recv[h, k].astype(F32) * factors[k]
        own_half.append(
            [merged[0:8, j : j + 128] for j in range(0, half, 128)]
        )
        for k in far_z:
            part = merged[k * 8 : (k + 1) * 8]
            low_send[h, k] = jnp.concatenate([part[:, 0:128], part[:, 128:256]], axis=0).astype(BF16)
            num_z[h][k] = send(
                low_send.at[h, k],
                low_recv.at[h, k],
                nz_send.at[h, k],
                nz_recv.at[h, k],
                along_z(-k),
            )

    for k in far_z[::-1]:
        low_stats[k].wait_recv()
    found = [low_stat_send[0]] + [low_stat_recv[k] for k in range(1, NZ)]
    tops = [f[:, 0:1] for f in found]
    top_z = functools.reduce(jnp.maximum, tops)
    factors = [jnp.broadcast_to(jnp.exp2(t - top_z), (8, 128)) for t in tops]
    total_z = sum(f[:, 64:65] * w for f, w in zip(found, factors))
    attended = []
    for h in range(2):
        for k in far_z[::-1]:
            num_z[h][k].wait_recv()
        for j in range(2):
            merged = own_half[h][j] * factors[0]
            for k in range(1, NZ):
                merged = merged + low_recv[h, k].astype(F32)[j * 8 : (j + 1) * 8] * factors[k]
            attended.append(merged / total_z)
    attended = jnp.concatenate(attended, axis=1)
    head = lax.rem(lax.broadcasted_iota(jnp.int32, attended.shape, 0), heads)
    spread = [jnp.where(head == i, attended, 0.0) for i in range(heads)]
    up_copy.wait()
    values = dot(
        jnp.concatenate(spread, axis=1).astype(BF16), w_up[...].reshape(heads * latent, -1)
    )

    own = pl.ds(pl.multiple_of(g * 8, 8), 8)
    head_values[own, :] = values.astype(BF16).astype(F32)
    moved = {}
    for k in range(1, NG):
        moved[k] = send(
            head_values.at[own], head_values.at[own], v_send.at[k], v_recv.at[k], along_g(k)
        )
    for k in range(1, NG):
        moved[k].wait_recv()
    wide = [head_values[pl.ds(i, tokens * NG, stride=heads), :] for i in range(heads)]
    terms = dot(jnp.concatenate(wide, axis=1).astype(BF16), w_placed[...])

    for i in range(NX):
        term_send[i] = terms[:, i * x_lanes : (i + 1) * x_lanes].astype(BF16)
    tx = {}
    for k in far_x:
        tx[k] = send(
            term_send.at[lax.rem(x + k, NX)],
            term_recv.at[k],
            tx_send.at[k],
            tx_recv.at[k],
            along_x(k),
        )
    summed = term_send[x].astype(F32)
    for k in far_x[::-1]:
        tx[k].wait_recv()
    for k in range(1, NX):
        summed = summed + term_recv[k].astype(F32)
    for i in range(x_lanes // 128):
        last_send[i] = summed[:, i * 128 : (i + 1) * 128].astype(BF16)
    per_tile = 128 // out_group
    tz = {}
    for k in far_z:
        tz[k] = send(
            last_send.at[lax.div(lax.rem(z + k, NZ), per_tile)],
            last_recv.at[k],
            tz_send.at[k],
            tz_recv.at[k],
            along_z(k),
        )
    final = last_send[lax.div(z, per_tile)].astype(F32)
    for k in far_z[::-1]:
        tz[k].wait_recv()
    for k in range(1, NZ):
        final = final + last_recv[k].astype(F32)
    place = lax.rem(z, per_tile)
    chosen = final
    for i in range(1, per_tile):
        chosen = jnp.where(place == i, pltpu.roll(final, 128 - i * out_group, 1), chosen)
    result[...] = chosen

    for group in (*q_z, *q_x, *relayed, stats, num_x[0], num_x[1], low_stats, num_z[0], num_z[1], moved, tx, tz):
        for copy in group.values():
            copy.wait_send()


def body(sizes, queries, cache, slot_page, lengths, w_uv, w_out):
    NX, NZ, NG, own_columns = sizes
    tokens, heads, width = queries.shape[1:]
    latent = w_uv.shape[1]
    half = latent // 2
    key_rows = cache.shape[1] * cache.shape[2]
    rows = NX * NZ * 8
    block = NZ * 8
    x_lanes = NZ * out_group
    sem = pltpu.SemaphoreType.DMA
    scratch = [
        pltpu.VMEM(queries.shape, BF16),
        pltpu.VMEM((8, 768), F32),
        pltpu.VMEM((NZ, 16, 384), BF16),
        pltpu.VMEM((rows, 640), BF16),
        pltpu.VMEM((key_rows, width), BF16),
        pltpu.SMEM(slot_page.shape, jnp.int32),
        pltpu.SMEM(lengths.shape, jnp.int32),
        pltpu.VMEM(w_uv.shape, BF16),
        pltpu.VMEM(w_out.shape, BF16),
        pltpu.VMEM((w_out.shape[0], NX * x_lanes), BF16),
        pltpu.VMEM((8, key_rows), F32),
        pltpu.VMEM((rows, key_rows), F32),
        pltpu.VMEM((rows, key_rows), BF16),
        pltpu.VMEM((rows, 128), F32),
        pltpu.VMEM((rows, 128), F32),
        pltpu.VMEM((2, rows, half), F32),
        pltpu.VMEM((2, rows, half), BF16),
        pltpu.VMEM((2, NX, block, half), BF16),
        pltpu.VMEM((NX, 8, 128), F32),
        pltpu.VMEM((NX, 8, 128), F32),
        pltpu.VMEM((NZ, 8, 128), F32),
        pltpu.VMEM((NZ, 8, 128), F32),
        pltpu.VMEM((2, NZ, 16, 128), BF16),
        pltpu.VMEM((2, NZ, 16, 128), BF16),
        pltpu.VMEM((NG * 8, 128), F32),
        pltpu.VMEM((NX, tokens * NG, x_lanes), BF16),
        pltpu.VMEM((NX, tokens * NG, x_lanes), BF16),
        pltpu.VMEM((x_lanes // 128, tokens * NG, 128), BF16),
        pltpu.VMEM((NZ, tokens * NG, 128), BF16),
        sem((5,)),
        sem((key_rows // step_keys,)),
        sem((2, NZ)),
        sem((2, NZ)),
        sem((2, NX)),
        sem((2, NX)),
        sem((NX,)),
        sem((NX,)),
        sem((2, NX)),
        sem((2, NX)),
        sem((NZ,)),
        sem((NZ,)),
        sem((2, NZ)),
        sem((2, NZ)),
        sem((NG,)),
        sem((NG,)),
        sem((NX,)),
        sem((NX,)),
        sem((NZ,)),
        sem((NZ,)),
    ]
    result = pl.pallas_call(
        functools.partial(kernel, sizes),
        out_shape=jax.ShapeDtypeStruct((tokens * NG, 128), F32),
        in_specs=[pl.BlockSpec(memory_space=pltpu.HBM)] * 6,
        out_specs=pl.BlockSpec(memory_space=pltpu.VMEM),
        scratch_shapes=scratch,
        compiler_params=pltpu.CompilerParams(
            collective_id=0, has_side_effects=True, vmem_limit_bytes=56 * 1024 * 1024
        ),
    )(queries, cache.reshape(key_rows, width), slot_page, lengths, w_uv, w_out)
    return result[:, 0:own_columns].astype(BF16).reshape(NG, tokens, own_columns)


def solution(mesh, NX=4):
    NG, pages = mesh.shape["group"], mesh.shape["page"]
    in_specs = (
        P("group", None, "page", None),
        P("group", "page", None, None),
        P("group", "page"),
        P("group"),
        P("page", None, None),
        P("page", "group"),
    )
    out_specs = P(None, None, ("group", "page"))

    def step(queries, cache, slot_page, lengths, w_uv, w_out):
        sizes = (NX, pages // NX, NG, w_out.shape[1] // pages)
        return body(sizes, queries, cache, slot_page, lengths, w_uv, w_out)

    return jax.shard_map(step, mesh=mesh, in_specs=in_specs, out_specs=out_specs, check_vma=False)
```

time: 413 us -> 54.7 us (0.13)
  blocking collectives: 286 us -> 0 us
  waiting for transfers between devices: 54.4 us -> 0 us
  Pallas kernels: 0 us -> 52.2 us
  other arithmetic: 40.8 us -> 0 us
  between operations: 14.9 us -> 0.66 us
  matrix products: 9.34 us -> 0 us
    all_gather x4 -> x0, blocking collectives: 147 us -> none  [the longest x2 82.7 us: combined_all(): everything = jax.tree.map(lambda part: lax.all_gather(part, axis), shard)]
    unnamed x1 -> x0, blocking collectives: 139 us -> none
    all_gather x1 -> x0, waiting for transfers between devices: 54.4 us -> none  [combined_all(): everything = jax.tree.map(lambda part: lax.all_gather(part, axis), shard)]
    pallas_call x0 -> x1, Pallas kernels: none -> 52.2 us  [body(): pl.pallas_call(functools.partial(kernel, sizes), out_shape=jax.ShapeDtype...]
    add x64 -> x0, other arithmetic: 38.3 us -> none  [the longest x31 37.6 us: join_partials(): left_part[2] * left_factor[:, None] + right_part[2] * right_factor[:, None]]
    dot_general x4 -> x0, matrix products: 9.34 us -> none  [the longest x1 6.2 us: body(): lax.dot_general(whole_query.reshape(-1, width), key_rows, (((1,), (1,)),...]
  transfers between devices with their start and end apart: 1 -> 0, of which waited for: 1 -> 0; matrix products, arithmetic and copies ran while one was open for 0% -> 0% of each run, Pallas kernels for 0% -> 0%
where the time goes in v1:
time: 54.7 us; the launch traced here: 54.2 us
  Pallas kernels  52.2 us (95%)
  local copies, waits for them, and re-layouts  1.29 us (2%)
  between operations  0.66 us (1%)
    pallas_call x1, Pallas kernels, body(): pl.pallas_call(functools.partial(kernel, sizes), out_shape=jax.ShapeDtype...  52.2 us
    slice x1, local copies, waits for them, and re-layouts, body(): result[:, 0:own_columns].astype(BF16).reshape(NG, tokens, own_columns)  1.29 us

profile of v1, /device:TPU:8, one launch (start us, length us, event | category | flops | bytes accessed | tf_op | source)
XLA Modules:
  0.0 54.2 jit_solution(12771712736488846246)
XLA Ops:
  0.7 52.2 %shard_map.64 = f32[16,128]{1,0:T(8,128)} custom-call(bf16[1,2,4,576]{3,2,1,0:T(4,128)(2,1)} %q_hbm.1, bf16[6144,576]{1,0:T(8,128)(2,1)} %bitcast.2, s32[1,96]{1,0:T(1,128)} %page_hbm.1, s32[1]{0:T(128)S(6)} %copy.7.length_hbm, bf16[4,512,128]{2,1,0:T(8,128)(2,1)} %up_hbm.1, bf16[512,896]{1,0:T(8,128)(2,1)} %out_hbm.1), custom_call_target="tpu_custom_call" | custom-call | tf_op jit(solution)/shard_map/pallas_call | solution.py:515
  52.9 1.3 %slice.7 = bf16[16,28]{1,0:T(8,128)(2,1)} slice(f32[16,128]{1,0:T(8,128)} %shard_map.64), slice={[0:16], [0:28]} | slice | bytes 1792 | tf_op jit(solution)/shard_map/slice | solution.py:525

commit v2 on v1

v2 whole, which is shorter than its diff:
```python
import functools

import jax
import jax.numpy as jnp
from jax import lax
from jax.experimental import pallas as pl
from jax.experimental.pallas import tpu as pltpu
from jax.sharding import PartitionSpec as P

MESH = pl.DeviceIdType.MESH
F32 = jnp.float32
BF16 = jnp.bfloat16
score_scale = 192.0 ** (-0.5)
log2_e = 1.4426950408889634
masked_fill = -(2.0**99)
out_group = 32
step_keys = 1024
tile_keys = 256


def dot(a, b, contract_b=0):
    return lax.dot_general(a, b, (((1,), (contract_b,)), ((), ())), preferred_element_type=F32)


def kernel(
    sizes,
    q_hbm,
    k_hbm,
    page_hbm,
    length_hbm,
    up_hbm,
    out_hbm,
    result,
    q_in,
    q_rows,
    q_packed,
    q_all,
    keys,
    pages,
    length,
    w_up,
    w_out,
    w_placed,
    bias,
    scores,
    probs,
    peaks,
    sums,
    numer,
    num_send,
    num_recv,
    stat_send,
    stat_recv,
    low_send,
    low_recv,
    head_values,
    term_send,
    term_recv,
    last_send,
    last_recv,
    local_sem,
    key_sem,
    qz_send,
    qz_recv,
    qx_send,
    qx_recv,
    st_send,
    st_recv,
    nx_send,
    nx_recv,
    nz_send,
    nz_recv,
    v_send,
    v_recv,
    tx_send,
    tx_recv,
    tz_send,
    tz_recv,
):
    NX, NZ, NG, own_columns = sizes
    width = q_in.shape[-1]
    latent = w_up.shape[1]
    half = latent // 2
    key_rows = keys.shape[0]
    rows = q_all.shape[0]
    block = rows // NX
    steps = key_rows // step_keys
    tokens, heads = q_in.shape[1], q_in.shape[2]

    g = lax.axis_index("group")
    page = lax.axis_index("page")
    x, z = lax.div(page, NZ), lax.rem(page, NZ)

    def along_x(k):
        return {"page": lax.rem(x + k + NX, NX) * NZ + z}

    def along_z(k):
        return {"page": x * NZ + lax.rem(z + k + NZ, NZ)}

    def along_g(k):
        return {"group": lax.rem(g + k + NG, NG)}

    def send(source, target, send_sem, recv_sem, device):
        copy = pltpu.make_async_remote_copy(
            src_ref=source,
            dst_ref=target,
            send_sem=send_sem,
            recv_sem=recv_sem,
            device_id=device,
            device_id_type=MESH,
        )
        copy.start()
        return copy

    def done(region, sem):
        pltpu.make_async_copy(region, region, sem).wait()

    far_z = sorted(range(1, NZ), key=lambda k: -min(k, NZ - k))
    far_x = sorted(range(1, NX), key=lambda k: -min(k, NX - k))

    barrier = pltpu.get_barrier_semaphore()
    for k in range(1, NX):
        pl.semaphore_signal(barrier, inc=1, device_id=along_x(k), device_id_type=MESH)
    for k in range(1, NZ):
        pl.semaphore_signal(barrier, inc=1, device_id=along_z(k), device_id_type=MESH)
    for k in range(1, NG):
        pl.semaphore_signal(barrier, inc=1, device_id=along_g(k), device_id_type=MESH)

    def local(source, target, sem):
        copy = pltpu.make_async_copy(source, target, sem)
        copy.start()
        return copy

    q_copy = local(q_hbm, q_in, local_sem.at[0])
    page_copy = local(page_hbm, pages, local_sem.at[1])
    length_copy = local(length_hbm, length, local_sem.at[2])
    out_copy = local(out_hbm, w_out, local_sem.at[3])
    key_copies = [
        local(
            k_hbm.at[pl.ds(c * step_keys, step_keys)],
            keys.at[pl.ds(c * step_keys, step_keys)],
            key_sem.at[c],
        )
        for c in range(steps)
    ]
    up_copy = local(up_hbm, w_up, local_sem.at[4])

    q_copy.wait()
    q_rows[:, 512:768] = jnp.zeros((8, 256), F32)
    for t in range(tokens):
        q_rows[t * heads : (t + 1) * heads, 0:width] = q_in[0, t].astype(F32)
    q_packed[0] = jnp.concatenate([q_rows[:, 0:384], q_rows[:, 384:768]], axis=0).astype(BF16)
    pl.semaphore_wait(barrier, NX + NZ + NG - 3)
    for k in far_z:
        send(q_packed.at[0], q_packed.at[k], qz_send, qz_recv, along_z(k))

    page_copy.wait()
    length_copy.wait()
    lane = lax.broadcasted_iota(jnp.int32, (8, 128), 1)
    token = lax.broadcasted_iota(jnp.int32, (8, 128), 0) // heads
    limit = length[0] - tokens + token
    for i in range(key_rows // 128):
        held = jnp.where(lane < 64, pages[0, 2 * i], pages[0, 2 * i + 1])
        position = held * 64 + lax.rem(lane, 64)
        bias[:, i * 128 : (i + 1) * 128] = jnp.where(position <= limit, 0.0, masked_fill)
    done(q_packed.at[pl.ds(1, NZ - 1)], qz_recv)
    for k in range(0, NZ, 2):
        pair = []
        for j in (k, k + 1):
            part = q_packed[j].astype(F32)
            pair.append(jnp.concatenate([part[0:8], part[8:16, 0:256]], axis=1))
        q_all[k * 8 : k * 8 + 16, :] = jnp.concatenate(pair, axis=0).astype(BF16)
    for k in far_x:
        send(
            q_all.at[pl.ds(0, block)],
            q_all.at[pl.ds(k * block, block)],
            qx_send,
            qx_recv,
            along_x(k),
        )

    x_columns = own_columns * NZ
    x_lanes = out_group * NZ
    out_copy.wait()
    place = lax.broadcasted_iota(jnp.int32, (1, x_lanes), 1)
    inside = lax.rem(place, out_group)
    wanted = lax.div(place, out_group) * own_columns + inside
    wanted = jnp.where(inside < own_columns, wanted, -(2**20))
    for i in range(NX):
        low = i * x_columns // 128 * 128
        high = min(-(-(i + 1) * x_columns // 128) * 128, w_out.shape[1])
        column = lax.broadcasted_iota(jnp.int32, (high - low, x_lanes), 0)
        pick = jnp.where(column == wanted + (i * x_columns - low), 1.0, 0.0).astype(BF16)
        w_placed[:, i * x_lanes : (i + 1) * x_lanes] = dot(w_out[:, low:high], pick).astype(BF16)
    done(q_packed.at[pl.ds(1, NZ - 1)], qz_send)
    for copy in key_copies:
        copy.wait()
    done(q_all.at[pl.ds(block, rows - block)], qx_recv)

    peaks[...] = jnp.full(peaks.shape, masked_fill, F32)

    @pl.loop(0, steps)
    def _(c):
        largest = peaks[...]
        for n in range(step_keys // tile_keys):
            at = pl.ds(pl.multiple_of(c * step_keys + n * tile_keys, tile_keys), tile_keys)
            s = dot(q_all[:, 0:width], keys[at, :], 1) * (score_scale * log2_e)
            s = s.reshape(rows // 8, 8, tile_keys) + bias[:, at][None]
            s = s.reshape(rows, tile_keys)
            scores[:, at] = s
            for j in range(0, tile_keys, 128):
                largest = jnp.maximum(largest, s[:, j : j + 128])
        peaks[...] = largest

    top = jnp.max(peaks[...], axis=1, keepdims=True)
    peaks[...] = jnp.broadcast_to(top, peaks.shape)
    sums[...] = jnp.zeros(sums.shape, F32)
    numer[...] = jnp.zeros(numer.shape, F32)

    @pl.loop(0, steps)
    def _(c):
        total = sums[...]
        top_here = peaks[...]
        pieces = []
        for n in range(step_keys // 128):
            at = pl.ds(pl.multiple_of(c * step_keys + n * 128, 128), 128)
            p = jnp.exp2(scores[:, at] - top_here)
            total = total + p
            p = p.astype(BF16)
            probs[:, at] = p
            pieces.append(p)
        sums[...] = total
        here = pl.ds(pl.multiple_of(c * step_keys, step_keys), step_keys)
        numer[0] += dot(jnp.concatenate(pieces, axis=1), keys[here, 0:half])

    total = jnp.broadcast_to(jnp.sum(sums[...], axis=1, keepdims=True), (rows, 128))
    sums[...] = total
    owner = lax.div(lax.broadcasted_iota(jnp.int32, (8, 128), 1), 8)
    for i in range(NX):
        tile = jnp.zeros((8, 128), F32)
        for v in range(NZ):
            at = pl.ds(i * block + v * 8, 8)
            tile = jnp.where(owner == v, peaks[at, :], tile)
            tile = jnp.where(owner == v + 8, sums[at, :], tile)
        stat_send[i] = tile
    for k in far_x:
        send(stat_send.at[k], stat_recv.at[k], st_send, st_recv, along_x(-k))

    def send_half(h):
        num_send[h] = numer[h].astype(BF16)
        for k in far_x:
            send(
                num_send.at[h, pl.ds(k * block, block)],
                num_recv.at[h, k],
                nx_send.at[h],
                nx_recv.at[h],
                along_x(-k),
            )

    send_half(0)

    @pl.loop(0, steps)
    def _(c):
        here = pl.ds(pl.multiple_of(c * step_keys, step_keys), step_keys)
        numer[1] += dot(probs[:, here], keys[here, half:latent])

    send_half(1)
    done(q_all.at[pl.ds(block, rows - block)], qx_send)

    done(stat_recv.at[pl.ds(1, NX - 1)], st_recv)
    found = [stat_send[0]] + [stat_recv[k] for k in range(1, NX)]
    factors = [[] for _ in found]
    z_stats = []
    for v in range(NZ):
        tops = [jnp.broadcast_to(f[:, 8 * v : 8 * v + 1], (8, 128)) for f in found]
        top_x = functools.reduce(jnp.maximum, tops)
        coarse = top_x.astype(BF16).astype(F32)
        top_x = coarse + (top_x - coarse).astype(BF16).astype(F32)
        total_x = jnp.zeros((8, 128), F32)
        for f, t, held in zip(found, tops, factors):
            held.append(jnp.exp2(t - top_x))
            total_x = total_x + f[:, 64 + 8 * v : 64 + 8 * v + 1] * held[v]
        z_stats.append(jnp.where(lane < 64, top_x, total_x))
        if v > 0:
            coarse = z_stats[v].astype(BF16).astype(F32)
            low_send[v, :, 128:256] = jnp.concatenate(
                [coarse, z_stats[v] - coarse], axis=0
            ).astype(BF16)
    factors = [
        jnp.concatenate([jnp.concatenate(held, axis=0)] * (half // 128), axis=1) for held in factors
    ]

    spans = ((0, 256), (256, 384))
    own_half = []
    for h in range(2):
        done(num_recv.at[h, pl.ds(1, NX - 1)], nx_recv.at[h])
        merged = numer[h, 0:block, :] * factors[0]
        for k in range(1, NX):
            merged = merged + num_recv[h, k].astype(F32) * factors[k]
        own_half.append([merged[0:8, j : j + 128] for j in range(0, half, 128)])
        low, high = spans[h]
        for k in far_z:
            part = merged[k * 8 : (k + 1) * 8]
            low_send[k, :, low : low + 128] = jnp.concatenate(
                [part[:, 0:128], part[:, 128:256]], axis=0
            ).astype(BF16)
            send(
                low_send.at[k, :, low:high],
                low_recv.at[k, :, low:high],
                nz_send.at[h],
                nz_recv.at[h],
                along_z(-k),
            )
    done(stat_recv.at[pl.ds(1, NX - 1)], st_send)
    for h in range(2):
        done(num_recv.at[h, pl.ds(1, NX - 1)], nx_send.at[h])

    done(low_recv.at[pl.ds(1, NZ - 1), :, 0:256], nz_recv.at[0])
    found = [z_stats[0]]
    for k in range(1, NZ):
        held = low_recv[k, :, 128:256].astype(F32)
        found.append(held[0:8] + held[8:16])
    tops = [jnp.broadcast_to(f[:, 0:1], (8, 128)) for f in found]
    top_z = functools.reduce(jnp.maximum, tops)
    factors = [jnp.exp2(t - top_z) for t in tops]
    total_z = sum(f[:, 64:65] * w for f, w in zip(found, factors))
    attended = []
    for h in range(2):
        if h == 1:
            done(low_recv.at[pl.ds(1, NZ - 1), :, 256:384], nz_recv.at[1])
        merged = [own * factors[0] for own in own_half[h]]
        for k in range(1, NZ):
            held = low_recv[k, :, spans[h][0] : spans[h][0] + 128].astype(F32)
            for j in range(2):
                merged[j] = merged[j] + held[j * 8 : (j + 1) * 8] * factors[k]
        attended += [m / total_z for m in merged]
    attended = jnp.concatenate(attended, axis=1)
    head = lax.rem(lax.broadcasted_iota(jnp.int32, attended.shape, 0), heads)
    spread = [jnp.where(head == i, attended, 0.0) for i in range(heads)]
    up_copy.wait()
    values = dot(
        jnp.concatenate(spread, axis=1).astype(BF16), w_up[...].reshape(heads * latent, -1)
    )

    own = pl.ds(pl.multiple_of(g * 8, 8), 8)
    head_values[own, :] = values.astype(BF16).astype(F32)
    for k in range(1, NG):
        send(head_values.at[own], head_values.at[own], v_send, v_recv, along_g(k))
    others = head_values.at[pl.ds(0, (NG - 1) * 8)]
    done(low_recv.at[pl.ds(1, NZ - 1), :, 0:256], nz_send.at[0])
    done(low_recv.at[pl.ds(1, NZ - 1), :, 256:384], nz_send.at[1])
    done(others, v_recv)
    wide = [head_values[pl.ds(i, tokens * NG, stride=heads), :] for i in range(heads)]
    terms = dot(jnp.concatenate(wide, axis=1).astype(BF16), w_placed[...])

    for i in range(NX):
        term_send[i] = terms[:, i * x_lanes : (i + 1) * x_lanes].astype(BF16)
    for k in far_x:
        send(term_send.at[lax.rem(x + k, NX)], term_recv.at[k], tx_send, tx_recv, along_x(k))
    done(others, v_send)
    summed = term_send[x].astype(F32)
    done(term_recv.at[pl.ds(1, NX - 1)], tx_recv)
    for k in range(1, NX):
        summed = summed + term_recv[k].astype(F32)
    for i in range(x_lanes // 128):
        last_send[i] = summed[:, i * 128 : (i + 1) * 128].astype(BF16)
    per_tile = 128 // out_group
    for k in far_z:
        send(
            last_send.at[lax.div(lax.rem(z + k, NZ), per_tile)],
            last_recv.at[k],
            tz_send,
            tz_recv,
            along_z(k),
        )
    done(term_recv.at[pl.ds(1, NX - 1)], tx_send)
    final = last_send[lax.div(z, per_tile)].astype(F32)
    done(last_recv.at[pl.ds(1, NZ - 1)], tz_recv)
    for k in range(1, NZ):
        final = final + last_recv[k].astype(F32)
    place = lax.rem(z, per_tile)
    chosen = final
    for i in range(1, per_tile):
        chosen = jnp.where(place == i, pltpu.roll(final, 128 - i * out_group, 1), chosen)
    result[...] = chosen
    done(last_recv.at[pl.ds(1, NZ - 1)], tz_send)


def body(sizes, queries, cache, slot_page, lengths, w_uv, w_out):
    NX, NZ, NG, own_columns = sizes
    tokens, heads, width = queries.shape[1:]
    latent = w_uv.shape[1]
    half = latent // 2
    key_rows = cache.shape[1] * cache.shape[2]
    rows = NX * NZ * 8
    block = NZ * 8
    x_lanes = NZ * out_group
    sem = pltpu.SemaphoreType.DMA
    scratch = [
        pltpu.VMEM(queries.shape, BF16),
        pltpu.VMEM((8, 768), F32),
        pltpu.VMEM((NZ, 16, 384), BF16),
        pltpu.VMEM((rows, 640), BF16),
        pltpu.VMEM((key_rows, width), BF16),
        pltpu.SMEM(slot_page.shape, jnp.int32),
        pltpu.SMEM(lengths.shape, jnp.int32),
        pltpu.VMEM(w_uv.shape, BF16),
        pltpu.VMEM(w_out.shape, BF16),
        pltpu.VMEM((w_out.shape[0], NX * x_lanes), BF16),
        pltpu.VMEM((8, key_rows), F32),
        pltpu.VMEM((rows, key_rows), F32),
        pltpu.VMEM((rows, key_rows), BF16),
        pltpu.VMEM((rows, 128), F32),
        pltpu.VMEM((rows, 128), F32),
        pltpu.VMEM((2, rows, half), F32),
        pltpu.VMEM((2, rows, half), BF16),
        pltpu.VMEM((2, NX, block, half), BF16),
        pltpu.VMEM((NX, 8, 128), F32),
        pltpu.VMEM((NX, 8, 128), F32),
        pltpu.VMEM((NZ, 16, 384), BF16),
        pltpu.VMEM((NZ, 16, 384), BF16),
        pltpu.VMEM((NG * 8, 128), F32),
        pltpu.VMEM((NX, tokens * NG, x_lanes), BF16),
        pltpu.VMEM((NX, tokens * NG, x_lanes), BF16),
        pltpu.VMEM((x_lanes // 128, tokens * NG, 128), BF16),
        pltpu.VMEM((NZ, tokens * NG, 128), BF16),
        sem((5,)),
        sem((key_rows // step_keys,)),
        sem,
        sem,
        sem,
        sem,
        sem,
        sem,
        sem((2,)),
        sem((2,)),
        sem((2,)),
        sem((2,)),
        sem,
        sem,
        sem,
        sem,
        sem,
        sem,
    ]
    result = pl.pallas_call(
        functools.partial(kernel, sizes),
        out_shape=jax.ShapeDtypeStruct((tokens * NG, 128), F32),
        in_specs=[pl.BlockSpec(memory_space=pltpu.HBM)] * 6,
        out_specs=pl.BlockSpec(memory_space=pltpu.VMEM),
        scratch_shapes=scratch,
        compiler_params=pltpu.CompilerParams(
            collective_id=0, has_side_effects=True, vmem_limit_bytes=56 * 1024 * 1024
        ),
    )(queries, cache.reshape(key_rows, width), slot_page, lengths, w_uv, w_out)
    return result[:, 0:own_columns].astype(BF16).reshape(NG, tokens, own_columns)


def solution(mesh, NX=4):
    NG, pages = mesh.shape["group"], mesh.shape["page"]
    in_specs = (
        P("group", None, "page", None),
        P("group", "page", None, None),
        P("group", "page"),
        P("group"),
        P("page", None, None),
        P("page", "group"),
    )
    out_specs = P(None, None, ("group", "page"))

    def step(queries, cache, slot_page, lengths, w_uv, w_out):
        sizes = (NX, pages // NX, NG, w_out.shape[1] // pages)
        return body(sizes, queries, cache, slot_page, lengths, w_uv, w_out)

    return jax.shard_map(step, mesh=mesh, in_specs=in_specs, out_specs=out_specs, check_vma=False)
```

time: 54.7 us -> 50.5 us (0.923)
  Pallas kernels: 52.2 us -> 47.8 us
    pallas_call x1, Pallas kernels: 52.2 us -> 47.8 us  [body(): pl.pallas_call(functools.partial(kernel, sizes), out_shape=jax.ShapeDtype...]
where the time goes in v2:
time: 50.5 us; the launch traced here: 49.8 us
  Pallas kernels  47.8 us (95%)
  local copies, waits for them, and re-layouts  1.29 us (3%)
  between operations  0.66 us (1%)
    pallas_call x1, Pallas kernels, body(): pl.pallas_call(functools.partial(kernel, sizes), out_shape=jax.ShapeDtype...  47.8 us
    slice x1, local copies, waits for them, and re-layouts, body(): result[:, 0:own_columns].astype(BF16).reshape(NG, tokens, own_columns)  1.29 us

profile of v2, /device:TPU:8, one launch (start us, length us, event | category | flops | bytes accessed | tf_op | source)
XLA Modules:
  0.0 49.8 jit_solution(4735389526953825672)
XLA Ops:
  0.7 47.8 %shard_map.64 = f32[16,128]{1,0:T(8,128)} custom-call(bf16[1,2,4,576]{3,2,1,0:T(4,128)(2,1)} %q_hbm.1, bf16[6144,576]{1,0:T(8,128)(2,1)} %bitcast.2, s32[1,96]{1,0:T(1,128)} %page_hbm.1, s32[1]{0:T(128)S(6)} %copy.7.length_hbm, bf16[4,512,128]{2,1,0:T(8,128)(2,1)} %up_hbm.1, bf16[512,896]{1,0:T(8,128)(2,1)} %out_hbm.1), custom_call_target="tpu_custom_call" | custom-call | tf_op jit(solution)/shard_map/pallas_call | solution.py:446
  48.5 1.3 %slice.7 = bf16[16,28]{1,0:T(8,128)(2,1)} slice(f32[16,128]{1,0:T(8,128)} %shard_map.64), slice={[0:16], [0:28]} | slice | bytes 1792 | tf_op jit(solution)/shard_map/slice | solution.py:456

commit v3 on v2

--- a/solution.py
+++ b/solution.py
@@ -44,8 +44,6 @@
     bias,
     scores,
     probs,
-    peaks,
-    sums,
     numer,
     num_send,
     num_recv,
@@ -149,35 +147,32 @@
     q_rows[:, 512:768] = jnp.zeros((8, 256), F32)
     for t in range(tokens):
         q_rows[t * heads : (t + 1) * heads, 0:width] = q_in[0, t].astype(F32)
-    q_packed[0] = jnp.concatenate([q_rows[:, 0:384], q_rows[:, 384:768]], axis=0).astype(BF16)
+    q_packed[0, 0] = jnp.concatenate([q_rows[:, 0:384], q_rows[:, 384:768]], axis=0).astype(BF16)
     pl.semaphore_wait(barrier, NX + NZ + NG - 3)
     for k in far_z:
-        send(q_packed.at[0], q_packed.at[k], qz_send, qz_recv, along_z(k))
+        send(q_packed.at[0, 0], q_packed.at[0, k], qz_send, qz_recv.at[k], along_z(k))
+
+    def forward(j):
+        for k in far_x:
+            send(q_packed.at[0, j], q_packed.at[k, j], qx_send, qx_recv, along_x(k))
+
+    forward(0)
 
     page_copy.wait()
     length_copy.wait()
     lane = lax.broadcasted_iota(jnp.int32, (8, 128), 1)
-    token = lax.broadcasted_iota(jnp.int32, (8, 128), 0) // heads
-    limit = length[0] - tokens + token
-    for i in range(key_rows // 128):
-        held = jnp.where(lane < 64, pages[0, 2 * i], pages[0, 2 * i + 1])
-        position = held * 64 + lax.rem(lane, 64)
-        bias[:, i * 128 : (i + 1) * 128] = jnp.where(position <= limit, 0.0, masked_fill)
-    done(q_packed.at[pl.ds(1, NZ - 1)], qz_recv)
-    for k in range(0, NZ, 2):
-        pair = []
-        for j in (k, k + 1):
-            part = q_packed[j].astype(F32)
-            pair.append(jnp.concatenate([part[0:8], part[8:16, 0:256]], axis=1))
-        q_all[k * 8 : k * 8 + 16, :] = jnp.concatenate(pair, axis=0).astype(BF16)
-    for k in far_x:
-        send(
-            q_all.at[pl.ds(0, block)],
-            q_all.at[pl.ds(k * block, block)],
-            qx_send,
-            qx_recv,
-            along_x(k),
-        )
+    spot = lax.broadcasted_iota(jnp.int32, (64, 128), 0)
+    token = lax.rem(lax.broadcasted_iota(jnp.int32, (64, 128), 1), 8) // heads
+    last = length[0] - tokens + token - spot
+
+    @pl.loop(0, key_rows // 64)
+    def _(i):
+        at = pl.ds(pl.multiple_of(i * 64, 64), 64)
+        bias[at, :] = jnp.where(pages[0, i] * 64 <= last, 0.0, masked_fill)
+
+    for k in far_z[::-1]:
+        done(q_packed.at[0, k], qz_recv.at[k])
+        forward(k)
 
     x_columns = own_columns * NZ
     x_lanes = out_group * NZ
@@ -192,56 +187,66 @@
         column = lax.broadcasted_iota(jnp.int32, (high - low, x_lanes), 0)
         pick = jnp.where(column == wanted + (i * x_columns - low), 1.0, 0.0).astype(BF16)
         w_placed[:, i * x_lanes : (i + 1) * x_lanes] = dot(w_out[:, low:high], pick).astype(BF16)
-    done(q_packed.at[pl.ds(1, NZ - 1)], qz_send)
-    for copy in key_copies:
-        copy.wait()
-    done(q_all.at[pl.ds(block, rows - block)], qx_recv)
-
-    peaks[...] = jnp.full(peaks.shape, masked_fill, F32)
-
-    @pl.loop(0, steps)
-    def _(c):
-        largest = peaks[...]
-        for n in range(step_keys // tile_keys):
-            at = pl.ds(pl.multiple_of(c * step_keys + n * tile_keys, tile_keys), tile_keys)
-            s = dot(q_all[:, 0:width], keys[at, :], 1) * (score_scale * log2_e)
-            s = s.reshape(rows // 8, 8, tile_keys) + bias[:, at][None]
-            s = s.reshape(rows, tile_keys)
-            scores[:, at] = s
-            for j in range(0, tile_keys, 128):
-                largest = jnp.maximum(largest, s[:, j : j + 128])
-        peaks[...] = largest
-
-    top = jnp.max(peaks[...], axis=1, keepdims=True)
-    peaks[...] = jnp.broadcast_to(top, peaks.shape)
-    sums[...] = jnp.zeros(sums.shape, F32)
-    numer[...] = jnp.zeros(numer.shape, F32)
-
-    @pl.loop(0, steps)
-    def _(c):
-        total = sums[...]
-        top_here = peaks[...]
-        pieces = []
-        for n in range(step_keys // 128):
-            at = pl.ds(pl.multiple_of(c * step_keys + n * 128, 128), 128)
-            p = jnp.exp2(scores[:, at] - top_here)
-            total = total + p
-            p = p.astype(BF16)
-            probs[:, at] = p
+    done(q_packed.at[0, pl.ds(1, NZ - 1)], qz_send)
+    done(q_packed.at[pl.ds(1, NX - 1)], qx_recv)
+    for i in range(NX):
+        for j in range(0, NZ, 2):
+            pair = []
+            for part in (q_packed[i, j].astype(F32), q_packed[i, j + 1].astype(F32)):
+                pair.append(jnp.concatenate([part[0:8], part[8:16, 0:256]], axis=1))
+            first = i * block + j * 8
+            q_all[first : first + 16, :] = jnp.concatenate(pair, axis=0).astype(BF16)
+
+    def as_column(row):
+        return jnp.broadcast_to(row, (128, rows)).T
+
+    def scaled(value, row):
+        return value * jnp.concatenate([as_column(row)] * (value.shape[1] // 128), axis=1)
+
+    def score_tile(c, n):
+        at = pl.ds(c * step_keys + n * tile_keys, tile_keys)
+        s = dot(keys[at, :], q_all[:, 0:width], 1) * (score_scale * log2_e)
+        s = s + jnp.concatenate([bias[at, :]] * (rows // 128), axis=1)
+        scores[c % 2, n * tile_keys : (n + 1) * tile_keys, :] = s
+        return jnp.max(s.reshape(-1, 8, rows), axis=0)
+
+    tiles = step_keys // tile_keys
+    key_copies[0].wait()
+    largest = functools.reduce(jnp.maximum, [score_tile(0, n) for n in range(tiles)])
+    tops = []
+    total = jnp.zeros((8, rows), F32)
+    for c in range(steps):
+        top = jnp.max(largest, axis=0, keepdims=True)
+        if c > 0:
+            top = jnp.maximum(top, tops[-1])
+            shrink = jnp.exp2(tops[-1] - top)
+            total = total * shrink
+        tops.append(top)
+        if c + 1 < steps:
+            key_copies[c + 1].wait()
+        found, pieces = [], []
+        for n in range(tiles):
+            if c + 1 < steps:
+                found.append(score_tile(c + 1, n))
+            p = jnp.exp2(scores[c % 2, n * tile_keys : (n + 1) * tile_keys, :] - top)
+            total = total + jnp.sum(p.reshape(-1, 8, rows), axis=0)
+            p = p.astype(BF16).T
+            probs[:, c * step_keys + n * tile_keys : c * step_keys + (n + 1) * tile_keys] = p
             pieces.append(p)
-        sums[...] = total
-        here = pl.ds(pl.multiple_of(c * step_keys, step_keys), step_keys)
-        numer[0] += dot(jnp.concatenate(pieces, axis=1), keys[here, 0:half])
-
-    total = jnp.broadcast_to(jnp.sum(sums[...], axis=1, keepdims=True), (rows, 128))
-    sums[...] = total
+        if found:
+            largest = functools.reduce(jnp.maximum, found)
+        part = dot(jnp.concatenate(pieces, axis=1), keys[pl.ds(c * step_keys, step_keys), 0:half])
+        numer[0] = part if c == 0 else scaled(numer[0], shrink) + part
+
+    top_column = as_column(top)
+    sum_column = as_column(jnp.sum(total, axis=0, keepdims=True))
     owner = lax.div(lax.broadcasted_iota(jnp.int32, (8, 128), 1), 8)
     for i in range(NX):
         tile = jnp.zeros((8, 128), F32)
         for v in range(NZ):
-            at = pl.ds(i * block + v * 8, 8)
-            tile = jnp.where(owner == v, peaks[at, :], tile)
-            tile = jnp.where(owner == v + 8, sums[at, :], tile)
+            first = i * block + v * 8
+            tile = jnp.where(owner == v, top_column[first : first + 8], tile)
+            tile = jnp.where(owner == v + 8, sum_column[first : first + 8], tile)
         stat_send[i] = tile
     for k in far_x:
         send(stat_send.at[k], stat_recv.at[k], st_send, st_recv, along_x(-k))
@@ -259,13 +264,15 @@
 
     send_half(0)
 
-    @pl.loop(0, steps)
-    def _(c):
-        here = pl.ds(pl.multiple_of(c * step_keys, step_keys), step_keys)
-        numer[1] += dot(probs[:, here], keys[here, half:latent])
+    for c in range(steps):
+        here = pl.ds(c * step_keys, step_keys)
+        part = dot(probs[:, here], keys[here, half:latent])
+        if c + 1 < steps:
+            part = scaled(part, jnp.exp2(tops[c] - top))
+        numer[1] = part if c == 0 else numer[1] + part
 
     send_half(1)
-    done(q_all.at[pl.ds(block, rows - block)], qx_send)
+    done(q_packed.at[pl.ds(1, NX - 1)], qx_send)
 
     done(stat_recv.at[pl.ds(1, NX - 1)], st_recv)
     found = [stat_send[0]] + [stat_recv[k] for k in range(1, NX)]
@@ -399,7 +406,7 @@
     scratch = [
         pltpu.VMEM(queries.shape, BF16),
         pltpu.VMEM((8, 768), F32),
-        pltpu.VMEM((NZ, 16, 384), BF16),
+        pltpu.VMEM((NX, NZ, 16, 384), BF16),
         pltpu.VMEM((rows, 640), BF16),
         pltpu.VMEM((key_rows, width), BF16),
         pltpu.SMEM(slot_page.shape, jnp.int32),
@@ -407,11 +414,9 @@
         pltpu.VMEM(w_uv.shape, BF16),
         pltpu.VMEM(w_out.shape, BF16),
         pltpu.VMEM((w_out.shape[0], NX * x_lanes), BF16),
-        pltpu.VMEM((8, key_rows), F32),
-        pltpu.VMEM((rows, key_rows), F32),
+        pltpu.VMEM((key_rows, 128), F32),
+        pltpu.VMEM((2, step_keys, rows), F32),
         pltpu.VMEM((rows, key_rows), BF16),
-        pltpu.VMEM((rows, 128), F32),
-        pltpu.VMEM((rows, 128), F32),
         pltpu.VMEM((2, rows, half), F32),
         pltpu.VMEM((2, rows, half), BF16),
         pltpu.VMEM((2, NX, block, half), BF16),
@@ -427,7 +432,7 @@
         sem((5,)),
         sem((key_rows // step_keys,)),
         sem,
-        sem,
+        sem((NZ,)),
         sem,
         sem,
         sem,

time: 50.5 us -> 47.6 us (0.943)
  Pallas kernels: 47.8 us -> 44.9 us
    pallas_call x1, Pallas kernels: 47.8 us -> 44.9 us  [body(): pl.pallas_call(functools.partial(kernel, sizes), out_shape=jax.ShapeDtype...]
where the time goes in v3:
time: 47.6 us; the launch traced here: 46.9 us
  Pallas kernels  44.9 us (94%)
  local copies, waits for them, and re-layouts  1.29 us (3%)
  between operations  0.66 us (1%)
    pallas_call x1, Pallas kernels, body(): pl.pallas_call(functools.partial(kernel, sizes), out_shape=jax.ShapeDtype...  44.9 us
    slice x1, local copies, waits for them, and re-layouts, body(): result[:, 0:own_columns].astype(BF16).reshape(NG, tokens, own_columns)  1.29 us

profile of v3, /device:TPU:8, one launch (start us, length us, event | category | flops | bytes accessed | tf_op | source)
XLA Modules:
  0.0 46.9 jit_solution(15557860352515778854)
XLA Ops:
  0.7 44.9 %shard_map.64 = f32[16,128]{1,0:T(8,128)} custom-call(bf16[1,2,4,576]{3,2,1,0:T(4,128)(2,1)} %q_hbm.1, bf16[6144,576]{1,0:T(8,128)(2,1)} %bitcast.2, s32[1,96]{1,0:T(1,128)} %page_hbm.1, s32[1]{0:T(128)S(6)} %copy.7.length_hbm, bf16[4,512,128]{2,1,0:T(8,128)(2,1)} %up_hbm.1, bf16[512,896]{1,0:T(8,128)(2,1)} %out_hbm.1), custom_call_target="tpu_custom_call" | custom-call | tf_op jit(solution)/shard_map/pallas_call | solution.py:451
  45.6 1.3 %slice.7 = bf16[16,28]{1,0:T(8,128)(2,1)} slice(f32[16,128]{1,0:T(8,128)} %shard_map.64), slice={[0:16], [0:28]} | slice | bytes 1792 | tf_op jit(solution)/shard_map/slice | solution.py:461

commit v4 on v3

--- a/solution.py
+++ b/solution.py
@@ -13,9 +13,10 @@
 score_scale = 192.0 ** (-0.5)
 log2_e = 1.4426950408889634
 masked_fill = -(2.0**99)
+lowest_top = -(2.0**20)
 out_group = 32
 step_keys = 1024
-tile_keys = 256
+tile_keys = 512
 
 
 def dot(a, b, contract_b=0):
@@ -41,7 +42,7 @@
     w_up,
     w_out,
     w_placed,
-    bias,
+    tails,
     scores,
     probs,
     numer,
@@ -144,7 +145,9 @@
     up_copy = local(up_hbm, w_up, local_sem.at[4])
 
     q_copy.wait()
-    q_rows[:, 512:768] = jnp.zeros((8, 256), F32)
+    place = lax.broadcasted_iota(jnp.int32, (8, 256), 1) + 512
+    owner = lax.broadcasted_iota(jnp.int32, (8, 256), 0) // heads
+    q_rows[:, 512:768] = jnp.where(place == width + owner, 1.0, 0.0)
     for t in range(tokens):
         q_rows[t * heads : (t + 1) * heads, 0:width] = q_in[0, t].astype(F32)
     q_packed[0, 0] = jnp.concatenate([q_rows[:, 0:384], q_rows[:, 384:768]], axis=0).astype(BF16)
@@ -161,14 +164,9 @@
     page_copy.wait()
     length_copy.wait()
     lane = lax.broadcasted_iota(jnp.int32, (8, 128), 1)
-    spot = lax.broadcasted_iota(jnp.int32, (64, 128), 0)
-    token = lax.rem(lax.broadcasted_iota(jnp.int32, (64, 128), 1), 8) // heads
-    last = length[0] - tokens + token - spot
-
-    @pl.loop(0, key_rows // 64)
-    def _(i):
-        at = pl.ds(pl.multiple_of(i * 64, 64), 64)
-        bias[at, :] = jnp.where(pages[0, i] * 64 <= last, 0.0, masked_fill)
+    spot = lax.broadcasted_iota(jnp.int32, (64, 64), 0)
+    token = lax.broadcasted_iota(jnp.int32, (64, 64), 1)
+    last = jnp.where(token < tokens, length[0] - tokens + token - spot, 2**30)
 
     for k in far_z[::-1]:
         done(q_packed.at[0, k], qz_recv.at[k])
@@ -188,6 +186,15 @@
         pick = jnp.where(column == wanted + (i * x_columns - low), 1.0, 0.0).astype(BF16)
         w_placed[:, i * x_lanes : (i + 1) * x_lanes] = dot(w_out[:, low:high], pick).astype(BF16)
     done(q_packed.at[0, pl.ds(1, NZ - 1)], qz_send)
+    for c, copy in enumerate(key_copies):
+        copy.wait()
+
+        @pl.loop(c * step_keys // 64, (c + 1) * step_keys // 64)
+        def _(i):
+            at = pl.ds(pl.multiple_of(i * 64, 64), 64)
+            mask = jnp.where(pages[0, i] * 64 <= last, 0.0, masked_fill).astype(BF16)
+            tails[at, :] = jnp.concatenate([keys[at, latent:width], mask], axis=1)
+
     done(q_packed.at[pl.ds(1, NX - 1)], qx_recv)
     for i in range(NX):
         for j in range(0, NZ, 2):
@@ -205,34 +212,30 @@
 
     def score_tile(c, n):
         at = pl.ds(c * step_keys + n * tile_keys, tile_keys)
-        s = dot(keys[at, :], q_all[:, 0:width], 1) * (score_scale * log2_e)
-        s = s + jnp.concatenate([bias[at, :]] * (rows // 128), axis=1)
+        wide = jnp.concatenate([keys[at, 0:latent], tails[at, :]], axis=1)
+        s = dot(wide, q_all[...], 1) * (score_scale * log2_e)
         scores[c % 2, n * tile_keys : (n + 1) * tile_keys, :] = s
         return jnp.max(s.reshape(-1, 8, rows), axis=0)
 
     tiles = step_keys // tile_keys
-    key_copies[0].wait()
     largest = functools.reduce(jnp.maximum, [score_tile(0, n) for n in range(tiles)])
-    tops = []
+    tops = [jnp.full((1, rows), lowest_top, F32)]
     total = jnp.zeros((8, rows), F32)
     for c in range(steps):
-        top = jnp.max(largest, axis=0, keepdims=True)
-        if c > 0:
-            top = jnp.maximum(top, tops[-1])
-            shrink = jnp.exp2(tops[-1] - top)
-            total = total * shrink
+        top = jnp.maximum(jnp.max(largest, axis=0, keepdims=True), tops[-1])
+        shrink = jnp.exp2(tops[-1] - top)
+        total = total * shrink
         tops.append(top)
-        if c + 1 < steps:
-            key_copies[c + 1].wait()
         found, pieces = [], []
         for n in range(tiles):
             if c + 1 < steps:
                 found.append(score_tile(c + 1, n))
-            p = jnp.exp2(scores[c % 2, n * tile_keys : (n + 1) * tile_keys, :] - top)
-            total = total + jnp.sum(p.reshape(-1, 8, rows), axis=0)
-            p = p.astype(BF16).T
-            probs[:, c * step_keys + n * tile_keys : c * step_keys + (n + 1) * tile_keys] = p
-            pieces.append(p)
+            for low in range(n * tile_keys, (n + 1) * tile_keys, 256):
+                p = jnp.exp2(scores[c % 2, low : low + 256, :] - top)
+                total = total + jnp.sum(p.reshape(-1, 8, rows), axis=0)
+                p = p.astype(BF16).T
+                probs[:, c * step_keys + low : c * step_keys + low + 256] = p
+                pieces.append(p)
         if found:
             largest = functools.reduce(jnp.maximum, found)
         part = dot(jnp.concatenate(pieces, axis=1), keys[pl.ds(c * step_keys, step_keys), 0:half])
@@ -268,7 +271,7 @@
         here = pl.ds(c * step_keys, step_keys)
         part = dot(probs[:, here], keys[here, half:latent])
         if c + 1 < steps:
-            part = scaled(part, jnp.exp2(tops[c] - top))
+            part = scaled(part, jnp.exp2(tops[c + 1] - top))
         numer[1] = part if c == 0 else numer[1] + part
 
     send_half(1)
@@ -414,7 +417,7 @@
         pltpu.VMEM(w_uv.shape, BF16),
         pltpu.VMEM(w_out.shape, BF16),
         pltpu.VMEM((w_out.shape[0], NX * x_lanes), BF16),
-        pltpu.VMEM((key_rows, 128), F32),
+        pltpu.VMEM((key_rows, 128), BF16),
         pltpu.VMEM((2, step_keys, rows), F32),
         pltpu.VMEM((rows, key_rows), BF16),
         pltpu.VMEM((2, rows, half), F32),

time: 47.6 us -> 49.9 us (1.048)
  Pallas kernels: 44.9 us -> 47.4 us
    pallas_call x1, Pallas kernels: 44.9 us -> 47.4 us  [body(): pl.pallas_call(functools.partial(kernel, sizes), out_shape=jax.ShapeDtype...]
where the time goes in v4:
time: 49.9 us; the launch traced here: 49.4 us
  Pallas kernels  47.4 us (95%)
  local copies, waits for them, and re-layouts  1.29 us (3%)
  between operations  0.66 us (1%)
    pallas_call x1, Pallas kernels, body(): pl.pallas_call(functools.partial(kernel, sizes), out_shape=jax.ShapeDtype...  47.4 us
    slice x1, local copies, waits for them, and re-layouts, body(): result[:, 0:own_columns].astype(BF16).reshape(NG, tokens, own_columns)  1.29 us

profile of v4, /device:TPU:8, one launch (start us, length us, event | category | flops | bytes accessed | tf_op | source)
XLA Modules:
  0.0 49.4 jit_solution(10950284929053208659)
XLA Ops:
  0.7 47.4 %shard_map.64 = f32[16,128]{1,0:T(8,128)} custom-call(bf16[1,2,4,576]{3,2,1,0:T(4,128)(2,1)} %q_hbm.1, bf16[6144,576]{1,0:T(8,128)(2,1)} %bitcast.2, s32[1,96]{1,0:T(1,128)} %page_hbm.1, s32[1]{0:T(128)S(6)} %copy.7.length_hbm, bf16[4,512,128]{2,1,0:T(8,128)(2,1)} %up_hbm.1, bf16[512,896]{1,0:T(8,128)(2,1)} %out_hbm.1), custom_call_target="tpu_custom_call" | custom-call | tf_op jit(solution)/shard_map/pallas_call | solution.py:454
  48.1 1.3 %slice.7 = bf16[16,28]{1,0:T(8,128)(2,1)} slice(f32[16,128]{1,0:T(8,128)} %shard_map.64), slice={[0:16], [0:28]} | slice | bytes 1792 | tf_op jit(solution)/shard_map/slice | solution.py:464

commit v5 on v4

--- a/solution.py
+++ b/solution.py
@@ -168,10 +168,6 @@
     token = lax.broadcasted_iota(jnp.int32, (64, 64), 1)
     last = jnp.where(token < tokens, length[0] - tokens + token - spot, 2**30)
 
-    for k in far_z[::-1]:
-        done(q_packed.at[0, k], qz_recv.at[k])
-        forward(k)
-
     x_columns = own_columns * NZ
     x_lanes = out_group * NZ
     out_copy.wait()
@@ -185,11 +181,16 @@
         column = lax.broadcasted_iota(jnp.int32, (high - low, x_lanes), 0)
         pick = jnp.where(column == wanted + (i * x_columns - low), 1.0, 0.0).astype(BF16)
         w_placed[:, i * x_lanes : (i + 1) * x_lanes] = dot(w_out[:, low:high], pick).astype(BF16)
+
+    for k in far_z[::-1]:
+        done(q_packed.at[0, k], qz_recv.at[k])
+        forward(k)
+
     done(q_packed.at[0, pl.ds(1, NZ - 1)], qz_send)
     for c, copy in enumerate(key_copies):
         copy.wait()
 
-        @pl.loop(c * step_keys // 64, (c + 1) * step_keys // 64)
+        @pl.loop(c * step_keys // 64, (c + 1) * step_keys // 64, unroll=8)
         def _(i):
             at = pl.ds(pl.multiple_of(i * 64, 64), 64)
             mask = jnp.where(pages[0, i] * 64 <= last, 0.0, masked_fill).astype(BF16)

time: 49.9 us -> 46.6 us (0.934)
  Pallas kernels: 47.4 us -> 44 us
    pallas_call x1, Pallas kernels: 47.4 us -> 44 us  [body(): pl.pallas_call(functools.partial(kernel, sizes), out_shape=jax.ShapeDtype...]
where the time goes in v5:
time: 46.6 us; the launch traced here: 45.9 us
  Pallas kernels  44 us (94%)
  local copies, waits for them, and re-layouts  1.29 us (3%)
  between operations  0.66 us (1%)
    pallas_call x1, Pallas kernels, body(): pl.pallas_call(functools.partial(kernel, sizes), out_shape=jax.ShapeDtype...  44 us
    slice x1, local copies, waits for them, and re-layouts, body(): result[:, 0:own_columns].astype(BF16).reshape(NG, tokens, own_columns)  1.29 us

profile of v5, /device:TPU:8, one launch (start us, length us, event | category | flops | bytes accessed | tf_op | source)
XLA Modules:
  0.0 45.9 jit_solution(17274621484701865943)
XLA Ops:
  0.7 44.0 %shard_map.64 = f32[16,128]{1,0:T(8,128)} custom-call(bf16[1,2,4,576]{3,2,1,0:T(4,128)(2,1)} %q_hbm.1, bf16[6144,576]{1,0:T(8,128)(2,1)} %bitcast.2, s32[1,96]{1,0:T(1,128)} %page_hbm.1, s32[1]{0:T(128)S(6)} %copy.7.length_hbm, bf16[4,512,128]{2,1,0:T(8,128)(2,1)} %up_hbm.1, bf16[512,896]{1,0:T(8,128)(2,1)} %out_hbm.1), custom_call_target="tpu_custom_call" | custom-call | tf_op jit(solution)/shard_map/pallas_call | solution.py:455
  44.6 1.3 %slice.7 = bf16[16,28]{1,0:T(8,128)(2,1)} slice(f32[16,128]{1,0:T(8,128)} %shard_map.64), slice={[0:16], [0:28]} | slice | bytes 1792 | tf_op jit(solution)/shard_map/slice | solution.py:465

commit v6 on v5

--- a/solution.py
+++ b/solution.py
@@ -17,6 +17,7 @@
 out_group = 32
 step_keys = 1024
 tile_keys = 512
+turned_early = 3
 
 
 def dot(a, b, contract_b=0):
@@ -46,6 +47,7 @@
     scores,
     probs,
     numer,
+    turned,
     num_send,
     num_recv,
     stat_send,
@@ -168,20 +170,6 @@
     token = lax.broadcasted_iota(jnp.int32, (64, 64), 1)
     last = jnp.where(token < tokens, length[0] - tokens + token - spot, 2**30)
 
-    x_columns = own_columns * NZ
-    x_lanes = out_group * NZ
-    out_copy.wait()
-    place = lax.broadcasted_iota(jnp.int32, (1, x_lanes), 1)
-    inside = lax.rem(place, out_group)
-    wanted = lax.div(place, out_group) * own_columns + inside
-    wanted = jnp.where(inside < own_columns, wanted, -(2**20))
-    for i in range(NX):
-        low = i * x_columns // 128 * 128
-        high = min(-(-(i + 1) * x_columns // 128) * 128, w_out.shape[1])
-        column = lax.broadcasted_iota(jnp.int32, (high - low, x_lanes), 0)
-        pick = jnp.where(column == wanted + (i * x_columns - low), 1.0, 0.0).astype(BF16)
-        w_placed[:, i * x_lanes : (i + 1) * x_lanes] = dot(w_out[:, low:high], pick).astype(BF16)
-
     for k in far_z[::-1]:
         done(q_packed.at[0, k], qz_recv.at[k])
         forward(k)
@@ -196,6 +184,12 @@
             mask = jnp.where(pages[0, i] * 64 <= last, 0.0, masked_fill).astype(BF16)
             tails[at, :] = jnp.concatenate([keys[at, latent:width], mask], axis=1)
 
+    def turn(c):
+        here = pl.ds(c * step_keys, step_keys)
+        turned[:, here] = keys[here, 0:latent].T
+
+    for c in range(turned_early):
+        turn(c)
     done(q_packed.at[pl.ds(1, NX - 1)], qx_recv)
     for i in range(NX):
         for j in range(0, NZ, 2):
@@ -207,9 +201,6 @@
 
     def as_column(row):
         return jnp.broadcast_to(row, (128, rows)).T
-
-    def scaled(value, row):
-        return value * jnp.concatenate([as_column(row)] * (value.shape[1] // 128), axis=1)
 
     def score_tile(c, n):
         at = pl.ds(c * step_keys + n * tile_keys, tile_keys)
@@ -234,13 +225,16 @@
             for low in range(n * tile_keys, (n + 1) * tile_keys, 256):
                 p = jnp.exp2(scores[c % 2, low : low + 256, :] - top)
                 total = total + jnp.sum(p.reshape(-1, 8, rows), axis=0)
-                p = p.astype(BF16).T
-                probs[:, c * step_keys + low : c * step_keys + low + 256] = p
+                p = p.astype(BF16)
+                probs[c * step_keys + low : c * step_keys + low + 256, :] = p
                 pieces.append(p)
         if found:
             largest = functools.reduce(jnp.maximum, found)
-        part = dot(jnp.concatenate(pieces, axis=1), keys[pl.ds(c * step_keys, step_keys), 0:half])
-        numer[0] = part if c == 0 else scaled(numer[0], shrink) + part
+        if turned_early <= c + 1 < steps:
+            turn(c + 1)
+        here = pl.ds(c * step_keys, step_keys)
+        part = dot(turned[0:half, here], jnp.concatenate(pieces, axis=0))
+        numer[0] = part if c == 0 else numer[0] * shrink + part
 
     top_column = as_column(top)
     sum_column = as_column(jnp.sum(total, axis=0, keepdims=True))
@@ -256,7 +250,7 @@
         send(stat_send.at[k], stat_recv.at[k], st_send, st_recv, along_x(-k))
 
     def send_half(h):
-        num_send[h] = numer[h].astype(BF16)
+        num_send[h] = numer[h].astype(BF16).T
         for k in far_x:
             send(
                 num_send.at[h, pl.ds(k * block, block)],
@@ -270,9 +264,9 @@
 
     for c in range(steps):
         here = pl.ds(c * step_keys, step_keys)
-        part = dot(probs[:, here], keys[here, half:latent])
+        part = dot(turned[half:latent, here], probs[here, :])
         if c + 1 < steps:
-            part = scaled(part, jnp.exp2(tops[c + 1] - top))
+            part = part * jnp.exp2(tops[c + 1] - top)
         numer[1] = part if c == 0 else numer[1] + part
 
     send_half(1)
@@ -305,7 +299,7 @@
     own_half = []
     for h in range(2):
         done(num_recv.at[h, pl.ds(1, NX - 1)], nx_recv.at[h])
-        merged = numer[h, 0:block, :] * factors[0]
+        merged = num_send[h, 0:block, :].astype(F32) * factors[0]
         for k in range(1, NX):
             merged = merged + num_recv[h, k].astype(F32) * factors[k]
         own_half.append([merged[0:8, j : j + 128] for j in range(0, half, 128)])
@@ -322,6 +316,20 @@
                 nz_recv.at[h],
                 along_z(-k),
             )
+    x_columns = own_columns * NZ
+    x_lanes = out_group * NZ
+    out_copy.wait()
+    place = lax.broadcasted_iota(jnp.int32, (1, x_lanes), 1)
+    inside = lax.rem(place, out_group)
+    wanted = lax.div(place, out_group) * own_columns + inside
+    wanted = jnp.where(inside < own_columns, wanted, -(2**20))
+    for i in range(NX):
+        low = i * x_columns // 128 * 128
+        high = min(-(-(i + 1) * x_columns // 128) * 128, w_out.shape[1])
+        column = lax.broadcasted_iota(jnp.int32, (high - low, x_lanes), 0)
+        pick = jnp.where(column == wanted + (i * x_columns - low), 1.0, 0.0).astype(BF16)
+        w_placed[:, i * x_lanes : (i + 1) * x_lanes] = dot(w_out[:, low:high], pick).astype(BF16)
+
     done(stat_recv.at[pl.ds(1, NX - 1)], st_send)
     for h in range(2):
         done(num_recv.at[h, pl.ds(1, NX - 1)], nx_send.at[h])
@@ -420,8 +428,9 @@
         pltpu.VMEM((w_out.shape[0], NX * x_lanes), BF16),
         pltpu.VMEM((key_rows, 128), BF16),
         pltpu.VMEM((2, step_keys, rows), F32),
-        pltpu.VMEM((rows, key_rows), BF16),
-        pltpu.VMEM((2, rows, half), F32),
+        pltpu.VMEM((key_rows, rows), BF16),
+        pltpu.VMEM((2, half, rows), F32),
+        pltpu.VMEM((latent, key_rows), BF16),
         pltpu.VMEM((2, rows, half), BF16),
         pltpu.VMEM((2, NX, block, half), BF16),
         pltpu.VMEM((NX, 8, 128), F32),

time: 46.6 us -> 47 us (level)
  no operation moved by 1% of the time
where the time goes in v6:
time: 47 us; the launch traced here: 46.3 us
  Pallas kernels  44.3 us (94%)
  local copies, waits for them, and re-layouts  1.29 us (3%)
  between operations  0.66 us (1%)
    pallas_call x1, Pallas kernels, body(): pl.pallas_call(functools.partial(kernel, sizes), out_shape=jax.ShapeDtype...  44.3 us
    slice x1, local copies, waits for them, and re-layouts, body(): result[:, 0:own_columns].astype(BF16).reshape(NG, tokens, own_columns)  1.29 us

profile of v6, /device:TPU:8, one launch (start us, length us, event | category | flops | bytes accessed | tf_op | source)
XLA Modules:
  0.0 46.3 jit_solution(6330352866699144186)
XLA Ops:
  0.7 44.3 %shard_map.64 = f32[16,128]{1,0:T(8,128)} custom-call(bf16[1,2,4,576]{3,2,1,0:T(4,128)(2,1)} %q_hbm.1, bf16[6144,576]{1,0:T(8,128)(2,1)} %bitcast.2, s32[1,96]{1,0:T(1,128)} %page_hbm.1, s32[1]{0:T(128)S(6)} %copy.7.length_hbm, bf16[4,512,128]{2,1,0:T(8,128)(2,1)} %up_hbm.1, bf16[512,896]{1,0:T(8,128)(2,1)} %out_hbm.1), custom_call_target="tpu_custom_call" | custom-call | tf_op jit(solution)/shard_map/pallas_call | solution.py:464
  45.0 1.3 %slice.7 = bf16[16,28]{1,0:T(8,128)(2,1)} slice(f32[16,128]{1,0:T(8,128)} %shard_map.64), slice={[0:16], [0:28]} | slice | bytes 1792 | tf_op jit(solution)/shard_map/slice | solution.py:474

commit v7 on v5

--- a/solution.py
+++ b/solution.py
@@ -115,15 +115,9 @@
         pltpu.make_async_copy(region, region, sem).wait()
 
     far_z = sorted(range(1, NZ), key=lambda k: -min(k, NZ - k))
+    order = [0] + far_z[::-1]
+    far_g = sorted(range(1, NG), key=lambda k: -min(k, NG - k))
     far_x = sorted(range(1, NX), key=lambda k: -min(k, NX - k))
-
-    barrier = pltpu.get_barrier_semaphore()
-    for k in range(1, NX):
-        pl.semaphore_signal(barrier, inc=1, device_id=along_x(k), device_id_type=MESH)
-    for k in range(1, NZ):
-        pl.semaphore_signal(barrier, inc=1, device_id=along_z(k), device_id_type=MESH)
-    for k in range(1, NG):
-        pl.semaphore_signal(barrier, inc=1, device_id=along_g(k), device_id_type=MESH)
 
     def local(source, target, sem):
         copy = pltpu.make_async_copy(source, target, sem)
@@ -131,6 +125,10 @@
         return copy
 
     q_copy = local(q_hbm, q_in, local_sem.at[0])
+    barrier = pltpu.get_barrier_semaphore()
+    peers = [along_z(k) for k in far_z] + [along_x(k) for k in far_x] + [along_g(k) for k in far_g]
+    for peer in peers:
+        pl.semaphore_signal(barrier, inc=1, device_id=peer, device_id_type=MESH)
     page_copy = local(page_hbm, pages, local_sem.at[1])
     length_copy = local(length_hbm, length, local_sem.at[2])
     out_copy = local(out_hbm, w_out, local_sem.at[3])
@@ -150,16 +148,10 @@
     q_rows[:, 512:768] = jnp.where(place == width + owner, 1.0, 0.0)
     for t in range(tokens):
         q_rows[t * heads : (t + 1) * heads, 0:width] = q_in[0, t].astype(F32)
-    q_packed[0, 0] = jnp.concatenate([q_rows[:, 0:384], q_rows[:, 384:768]], axis=0).astype(BF16)
-    pl.semaphore_wait(barrier, NX + NZ + NG - 3)
+    q_packed[0] = jnp.concatenate([q_rows[:, 0:384], q_rows[:, 384:768]], axis=0).astype(BF16)
+    pl.semaphore_wait(barrier, len(peers))
     for k in far_z:
-        send(q_packed.at[0, 0], q_packed.at[0, k], qz_send, qz_recv.at[k], along_z(k))
-
-    def forward(j):
-        for k in far_x:
-            send(q_packed.at[0, j], q_packed.at[k, j], qx_send, qx_recv, along_x(k))
-
-    forward(0)
+        send(q_packed.at[0], q_packed.at[k], qz_send, qz_recv.at[k], along_z(k))
 
     page_copy.wait()
     length_copy.wait()
@@ -168,25 +160,6 @@
     token = lax.broadcasted_iota(jnp.int32, (64, 64), 1)
     last = jnp.where(token < tokens, length[0] - tokens + token - spot, 2**30)
 
-    x_columns = own_columns * NZ
-    x_lanes = out_group * NZ
-    out_copy.wait()
-    place = lax.broadcasted_iota(jnp.int32, (1, x_lanes), 1)
-    inside = lax.rem(place, out_group)
-    wanted = lax.div(place, out_group) * own_columns + inside
-    wanted = jnp.where(inside < own_columns, wanted, -(2**20))
-    for i in range(NX):
-        low = i * x_columns // 128 * 128
-        high = min(-(-(i + 1) * x_columns // 128) * 128, w_out.shape[1])
-        column = lax.broadcasted_iota(jnp.int32, (high - low, x_lanes), 0)
-        pick = jnp.where(column == wanted + (i * x_columns - low), 1.0, 0.0).astype(BF16)
-        w_placed[:, i * x_lanes : (i + 1) * x_lanes] = dot(w_out[:, low:high], pick).astype(BF16)
-
-    for k in far_z[::-1]:
-        done(q_packed.at[0, k], qz_recv.at[k])
-        forward(k)
-
-    done(q_packed.at[0, pl.ds(1, NZ - 1)], qz_send)
     for c, copy in enumerate(key_copies):
         copy.wait()
 
@@ -196,14 +169,25 @@
             mask = jnp.where(pages[0, i] * 64 <= last, 0.0, masked_fill).astype(BF16)
             tails[at, :] = jnp.concatenate([keys[at, latent:width], mask], axis=1)
 
-    done(q_packed.at[pl.ds(1, NX - 1)], qx_recv)
-    for i in range(NX):
-        for j in range(0, NZ, 2):
-            pair = []
-            for part in (q_packed[i, j].astype(F32), q_packed[i, j + 1].astype(F32)):
-                pair.append(jnp.concatenate([part[0:8], part[8:16, 0:256]], axis=1))
-            first = i * block + j * 8
-            q_all[first : first + 16, :] = jnp.concatenate(pair, axis=0).astype(BF16)
+    for n in range(0, NZ, 2):
+        pair = []
+        for j in order[n : n + 2]:
+            if j > 0:
+                done(q_packed.at[j], qz_recv.at[j])
+            part = q_packed[j].astype(F32)
+            pair.append(jnp.concatenate([part[0:8], part[8:16, 0:256]], axis=1))
+        q_all[n * 8 : n * 8 + 16, :] = jnp.concatenate(pair, axis=0).astype(BF16)
+        for k in far_x:
+            send(
+                q_all.at[pl.ds(n * 8, 16)],
+                q_all.at[pl.ds(k * block + n * 8, 16)],
+                qx_send,
+                qx_recv,
+                along_x(k),
+            )
+    done(q_packed.at[pl.ds(1, NZ - 1)], qz_send)
+
+    done(q_all.at[pl.ds(block, rows - block)], qx_recv)
 
     def as_column(row):
         return jnp.broadcast_to(row, (128, rows)).T
@@ -276,7 +260,7 @@
         numer[1] = part if c == 0 else numer[1] + part
 
     send_half(1)
-    done(q_packed.at[pl.ds(1, NX - 1)], qx_send)
+    done(q_all.at[pl.ds(block, rows - block)], qx_send)
 
     done(stat_recv.at[pl.ds(1, NX - 1)], st_recv)
     found = [stat_send[0]] + [stat_recv[k] for k in range(1, NX)]
@@ -294,7 +278,7 @@
         z_stats.append(jnp.where(lane < 64, top_x, total_x))
         if v > 0:
             coarse = z_stats[v].astype(BF16).astype(F32)
-            low_send[v, :, 128:256] = jnp.concatenate(
+            low_send[order[v], :, 128:256] = jnp.concatenate(
                 [coarse, z_stats[v] - coarse], axis=0
             ).astype(BF16)
     factors = [
@@ -311,7 +295,7 @@
         own_half.append([merged[0:8, j : j + 128] for j in range(0, half, 128)])
         low, high = spans[h]
         for k in far_z:
-            part = merged[k * 8 : (k + 1) * 8]
+            part = merged[order.index(k) * 8 : (order.index(k) + 1) * 8]
             low_send[k, :, low : low + 128] = jnp.concatenate(
                 [part[:, 0:128], part[:, 128:256]], axis=0
             ).astype(BF16)
@@ -322,6 +306,20 @@
                 nz_recv.at[h],
                 along_z(-k),
             )
+    x_columns = own_columns * NZ
+    x_lanes = out_group * NZ
+    out_copy.wait()
+    place = lax.broadcasted_iota(jnp.int32, (1, x_lanes), 1)
+    inside = lax.rem(place, out_group)
+    wanted = lax.div(place, out_group) * own_columns + inside
+    wanted = jnp.where(inside < own_columns, wanted, -(2**20))
+    for i in range(NX):
+        low = i * x_columns // 128 * 128
+        high = min(-(-(i + 1) * x_columns // 128) * 128, w_out.shape[1])
+        column = lax.broadcasted_iota(jnp.int32, (high - low, x_lanes), 0)
+        pick = jnp.where(column == wanted + (i * x_columns - low), 1.0, 0.0).astype(BF16)
+        w_placed[:, i * x_lanes : (i + 1) * x_lanes] = dot(w_out[:, low:high], pick).astype(BF16)
+
     done(stat_recv.at[pl.ds(1, NX - 1)], st_send)
     for h in range(2):
         done(num_recv.at[h, pl.ds(1, NX - 1)], nx_send.at[h])
@@ -355,7 +353,7 @@
 
     own = pl.ds(pl.multiple_of(g * 8, 8), 8)
     head_values[own, :] = values.astype(BF16).astype(F32)
-    for k in range(1, NG):
+    for k in far_g:
         send(head_values.at[own], head_values.at[own], v_send, v_recv, along_g(k))
     others = head_values.at[pl.ds(0, (NG - 1) * 8)]
     done(low_recv.at[pl.ds(1, NZ - 1), :, 0:256], nz_send.at[0])
@@ -410,7 +408,7 @@
     scratch = [
         pltpu.VMEM(queries.shape, BF16),
         pltpu.VMEM((8, 768), F32),
-        pltpu.VMEM((NX, NZ, 16, 384), BF16),
+        pltpu.VMEM((NZ, 16, 384), BF16),
         pltpu.VMEM((rows, 640), BF16),
         pltpu.VMEM((key_rows, width), BF16),
         pltpu.SMEM(slot_page.shape, jnp.int32),

time: 46.6 us -> 46.3 us (level)
  no operation moved by 1% of the time
where the time goes in v7:
time: 46.3 us; the launch traced here: 45.8 us
  Pallas kernels  43.8 us (95%)
  local copies, waits for them, and re-layouts  1.29 us (3%)
  between operations  0.66 us (1%)
    pallas_call x1, Pallas kernels, body(): pl.pallas_call(functools.partial(kernel, sizes), out_shape=jax.ShapeDtype...  43.8 us
    slice x1, local copies, waits for them, and re-layouts, body(): result[:, 0:own_columns].astype(BF16).reshape(NG, tokens, own_columns)  1.29 us

profile of v7, /device:TPU:8, one launch (start us, length us, event | category | flops | bytes accessed | tf_op | source)
XLA Modules:
  0.0 45.8 jit_solution(7755401345136526835)
XLA Ops:
  0.7 43.8 %shard_map.64 = f32[16,128]{1,0:T(8,128)} custom-call(bf16[1,2,4,576]{3,2,1,0:T(4,128)(2,1)} %q_hbm.1, bf16[6144,576]{1,0:T(8,128)(2,1)} %bitcast.2, s32[1,96]{1,0:T(1,128)} %page_hbm.1, s32[1]{0:T(128)S(6)} %copy.7.length_hbm, bf16[4,512,128]{2,1,0:T(8,128)(2,1)} %up_hbm.1, bf16[512,896]{1,0:T(8,128)(2,1)} %out_hbm.1), custom_call_target="tpu_custom_call" | custom-call | tf_op jit(solution)/shard_map/pallas_call | solution.py:453
  44.5 1.3 %slice.7 = bf16[16,28]{1,0:T(8,128)(2,1)} slice(f32[16,128]{1,0:T(8,128)} %shard_map.64), slice={[0:16], [0:28]} | slice | bytes 1792 | tf_op jit(solution)/shard_map/slice | solution.py:463

commit v8 on v7

--- a/solution.py
+++ b/solution.py
@@ -16,7 +16,7 @@
 lowest_top = -(2.0**20)
 out_group = 32
 step_keys = 1024
-tile_keys = 512
+tile_keys = 256
 
 
 def dot(a, b, contract_b=0):
@@ -45,6 +45,7 @@
     tails,
     scores,
     probs,
+    tops,
     numer,
     num_send,
     num_recv,
@@ -189,45 +190,46 @@
 
     done(q_all.at[pl.ds(block, rows - block)], qx_recv)
 
-    def as_column(row):
-        return jnp.broadcast_to(row, (128, rows)).T
-
-    def scaled(value, row):
-        return value * jnp.concatenate([as_column(row)] * (value.shape[1] // 128), axis=1)
+    def columns(value, width):
+        return jnp.concatenate([value] * (width // 128), axis=1)
 
     def score_tile(c, n):
         at = pl.ds(c * step_keys + n * tile_keys, tile_keys)
         wide = jnp.concatenate([keys[at, 0:latent], tails[at, :]], axis=1)
-        s = dot(wide, q_all[...], 1) * (score_scale * log2_e)
-        scores[c % 2, n * tile_keys : (n + 1) * tile_keys, :] = s
-        return jnp.max(s.reshape(-1, 8, rows), axis=0)
+        s = dot(q_all[...], wide, 1) * (score_scale * log2_e)
+        scores[c % 2, :, n * tile_keys : (n + 1) * tile_keys] = s
+        return functools.reduce(
+            jnp.maximum, [s[:, j : j + 128] for j in range(0, tile_keys, 128)]
+        )
 
     tiles = step_keys // tile_keys
     largest = functools.reduce(jnp.maximum, [score_tile(0, n) for n in range(tiles)])
-    tops = [jnp.full((1, rows), lowest_top, F32)]
-    total = jnp.zeros((8, rows), F32)
+    total = jnp.zeros((rows, 128), F32)
     for c in range(steps):
-        top = jnp.maximum(jnp.max(largest, axis=0, keepdims=True), tops[-1])
-        shrink = jnp.exp2(tops[-1] - top)
-        total = total * shrink
-        tops.append(top)
+        top = jnp.broadcast_to(jnp.max(largest, axis=1, keepdims=True), (rows, 128))
+        if c == 0:
+            tops[c] = jnp.maximum(top, lowest_top)
+        else:
+            tops[c] = jnp.maximum(top, tops[c - 1])
+            shrink = jnp.exp2(tops[c - 1] - tops[c])
+            total = total * shrink
         found, pieces = [], []
         for n in range(tiles):
             if c + 1 < steps:
                 found.append(score_tile(c + 1, n))
-            for low in range(n * tile_keys, (n + 1) * tile_keys, 256):
-                p = jnp.exp2(scores[c % 2, low : low + 256, :] - top)
-                total = total + jnp.sum(p.reshape(-1, 8, rows), axis=0)
-                p = p.astype(BF16).T
-                probs[:, c * step_keys + low : c * step_keys + low + 256] = p
+            for low in range(n * tile_keys, (n + 1) * tile_keys, 128):
+                p = jnp.exp2(scores[c % 2, :, low : low + 128] - tops[c])
+                total = total + p
+                p = p.astype(BF16)
+                probs[:, c * step_keys + low : c * step_keys + low + 128] = p
                 pieces.append(p)
         if found:
             largest = functools.reduce(jnp.maximum, found)
         part = dot(jnp.concatenate(pieces, axis=1), keys[pl.ds(c * step_keys, step_keys), 0:half])
-        numer[0] = part if c == 0 else scaled(numer[0], shrink) + part
-
-    top_column = as_column(top)
-    sum_column = as_column(jnp.sum(total, axis=0, keepdims=True))
+        numer[0] = part if c == 0 else numer[0] * columns(shrink, half) + part
+
+    top_column = tops[steps - 1]
+    sum_column = jnp.broadcast_to(jnp.sum(total, axis=1, keepdims=True), (rows, 128))
     owner = lax.div(lax.broadcasted_iota(jnp.int32, (8, 128), 1), 8)
     for i in range(NX):
         tile = jnp.zeros((8, 128), F32)
@@ -256,7 +258,7 @@
         here = pl.ds(c * step_keys, step_keys)
         part = dot(probs[:, here], keys[here, half:latent])
         if c + 1 < steps:
-            part = scaled(part, jnp.exp2(tops[c + 1] - top))
+            part = part * columns(jnp.exp2(tops[c] - tops[steps - 1]), half)
         numer[1] = part if c == 0 else numer[1] + part
 
     send_half(1)
@@ -267,12 +269,12 @@
     factors = [[] for _ in found]
     z_stats = []
     for v in range(NZ):
-        tops = [jnp.broadcast_to(f[:, 8 * v : 8 * v + 1], (8, 128)) for f in found]
-        top_x = functools.reduce(jnp.maximum, tops)
+        peaks = [jnp.broadcast_to(f[:, 8 * v : 8 * v + 1], (8, 128)) for f in found]
+        top_x = functools.reduce(jnp.maximum, peaks)
         coarse = top_x.astype(BF16).astype(F32)
         top_x = coarse + (top_x - coarse).astype(BF16).astype(F32)
         total_x = jnp.zeros((8, 128), F32)
-        for f, t, held in zip(found, tops, factors):
+        for f, t, held in zip(found, peaks, factors):
             held.append(jnp.exp2(t - top_x))
             total_x = total_x + f[:, 64 + 8 * v : 64 + 8 * v + 1] * held[v]
         z_stats.append(jnp.where(lane < 64, top_x, total_x))
@@ -329,9 +331,9 @@
     for k in range(1, NZ):
         held = low_recv[k, :, 128:256].astype(F32)
         found.append(held[0:8] + held[8:16])
-    tops = [jnp.broadcast_to(f[:, 0:1], (8, 128)) for f in found]
-    top_z = functools.reduce(jnp.maximum, tops)
-    factors = [jnp.exp2(t - top_z) for t in tops]
+    peaks = [jnp.broadcast_to(f[:, 0:1], (8, 128)) for f in found]
+    top_z = functools.reduce(jnp.maximum, peaks)
+    factors = [jnp.exp2(t - top_z) for t in peaks]
     total_z = sum(f[:, 64:65] * w for f, w in zip(found, factors))
     attended = []
     for h in range(2):
@@ -417,8 +419,9 @@
         pltpu.VMEM(w_out.shape, BF16),
         pltpu.VMEM((w_out.shape[0], NX * x_lanes), BF16),
         pltpu.VMEM((key_rows, 128), BF16),
-        pltpu.VMEM((2, step_keys, rows), F32),
+        pltpu.VMEM((2, rows, step_keys), F32),
         pltpu.VMEM((rows, key_rows), BF16),
+        pltpu.VMEM((key_rows // step_keys, rows, 128), F32),
         pltpu.VMEM((2, rows, half), F32),
         pltpu.VMEM((2, rows, half), BF16),
         pltpu.VMEM((2, NX, block, half), BF16),

time: 46.3 us -> 46.4 us (level)
  no operation moved by 1% of the time
where the time goes in v8:
time: 46.4 us; the launch traced here: 45.9 us
  Pallas kernels  44 us (95%)
  local copies, waits for them, and re-layouts  1.29 us (3%)
  between operations  0.66 us (1%)
    pallas_call x1, Pallas kernels, body(): pl.pallas_call(functools.partial(kernel, sizes), out_shape=jax.ShapeDtype...  44 us
    slice x1, local copies, waits for them, and re-layouts, body(): result[:, 0:own_columns].astype(BF16).reshape(NG, tokens, own_columns)  1.29 us

profile of v8, /device:TPU:8, one launch (start us, length us, event | category | flops | bytes accessed | tf_op | source)
XLA Modules:
  0.0 45.9 jit_solution(12867653726007428998)
XLA Ops:
  0.7 44.0 %shard_map.64 = f32[16,128]{1,0:T(8,128)} custom-call(bf16[1,2,4,576]{3,2,1,0:T(4,128)(2,1)} %q_hbm.1, bf16[6144,576]{1,0:T(8,128)(2,1)} %bitcast.2, s32[1,96]{1,0:T(1,128)} %page_hbm.1, s32[1]{0:T(128)S(6)} %copy.7.length_hbm, bf16[4,512,128]{2,1,0:T(8,128)(2,1)} %up_hbm.1, bf16[512,896]{1,0:T(8,128)(2,1)} %out_hbm.1), custom_call_target="tpu_custom_call" | custom-call | tf_op jit(solution)/shard_map/pallas_call | solution.py:456
  44.6 1.3 %slice.7 = bf16[16,28]{1,0:T(8,128)(2,1)} slice(f32[16,128]{1,0:T(8,128)} %shard_map.64), slice={[0:16], [0:28]} | slice | bytes 1792 | tf_op jit(solution)/shard_map/slice | solution.py:466

commit v9 on v8

--- a/solution.py
+++ b/solution.py
@@ -15,7 +15,7 @@
 masked_fill = -(2.0**99)
 lowest_top = -(2.0**20)
 out_group = 32
-step_keys = 1024
+step_keys = 512
 tile_keys = 256
 
 
@@ -218,9 +218,8 @@
             if c + 1 < steps:
                 found.append(score_tile(c + 1, n))
             for low in range(n * tile_keys, (n + 1) * tile_keys, 128):
-                p = jnp.exp2(scores[c % 2, :, low : low + 128] - tops[c])
-                total = total + p
-                p = p.astype(BF16)
+                p = jnp.exp2((scores[c % 2, :, low : low + 128] - tops[c]).astype(BF16))
+                total = total + p.astype(F32)
                 probs[:, c * step_keys + low : c * step_keys + low + 128] = p
                 pieces.append(p)
         if found:

time: 46.4 us -> 46.1 us (level)
  no operation moved by 1% of the time
where the time goes in v9:
time: 46.1 us; the launch traced here: 45.6 us
  Pallas kernels  43.6 us (95%)
  local copies, waits for them, and re-layouts  1.29 us (3%)
  between operations  0.66 us (1%)
    pallas_call x1, Pallas kernels, body(): pl.pallas_call(functools.partial(kernel, sizes), out_shape=jax.ShapeDtype...  43.6 us
    slice x1, local copies, waits for them, and re-layouts, body(): result[:, 0:own_columns].astype(BF16).reshape(NG, tokens, own_columns)  1.29 us

profile of v9, /device:TPU:8, one launch (start us, length us, event | category | flops | bytes accessed | tf_op | source)
XLA Modules:
  0.0 45.6 jit_solution(12654895750506428722)
XLA Ops:
  0.7 43.6 %shard_map.64 = f32[16,128]{1,0:T(8,128)} custom-call(bf16[1,2,4,576]{3,2,1,0:T(4,128)(2,1)} %q_hbm.1, bf16[6144,576]{1,0:T(8,128)(2,1)} %bitcast.2, s32[1,96]{1,0:T(1,128)} %page_hbm.1, s32[1]{0:T(128)S(6)} %copy.7.length_hbm, bf16[4,512,128]{2,1,0:T(8,128)(2,1)} %up_hbm.1, bf16[512,896]{1,0:T(8,128)(2,1)} %out_hbm.1), custom_call_target="tpu_custom_call" | custom-call | tf_op jit(solution)/shard_map/pallas_call | solution.py:455
  44.3 1.3 %slice.7 = bf16[16,28]{1,0:T(8,128)(2,1)} slice(f32[16,128]{1,0:T(8,128)} %shard_map.64), slice={[0:16], [0:28]} | slice | bytes 1792 | tf_op jit(solution)/shard_map/slice | solution.py:465

commit v10 on v9

--- a/solution.py
+++ b/solution.py
@@ -392,7 +392,7 @@
     chosen = final
     for i in range(1, per_tile):
         chosen = jnp.where(place == i, pltpu.roll(final, 128 - i * out_group, 1), chosen)
-    result[...] = chosen
+    result[...] = chosen.astype(BF16)
     done(last_recv.at[pl.ds(1, NZ - 1)], tz_send)
 
 
@@ -454,15 +454,15 @@
     ]
     result = pl.pallas_call(
         functools.partial(kernel, sizes),
-        out_shape=jax.ShapeDtypeStruct((tokens * NG, 128), F32),
+        out_shape=jax.ShapeDtypeStruct((tokens * NG, 128), BF16),
         in_specs=[pl.BlockSpec(memory_space=pltpu.HBM)] * 6,
         out_specs=pl.BlockSpec(memory_space=pltpu.VMEM),
         scratch_shapes=scratch,
         compiler_params=pltpu.CompilerParams(
-            collective_id=0, has_side_effects=True, vmem_limit_bytes=56 * 1024 * 1024
+            collective_id=0, has_side_effects=True, vmem_limit_bytes=55220 * 1024
         ),
     )(queries, cache.reshape(key_rows, width), slot_page, lengths, w_uv, w_out)
-    return result[:, 0:own_columns].astype(BF16).reshape(NG, tokens, own_columns)
+    return result[:, 0:own_columns].reshape(NG, tokens, own_columns)
 
 
 def solution(mesh, NX=4):

time: 46.1 us -> 45.3 us (0.983)
  Pallas kernels: 43.6 us -> 42.9 us
    slice x1 -> x0, local copies, waits for them, and re-layouts: 1.29 us -> none  [body(): result[:, 0:own_columns].astype(BF16).reshape(NG, tokens, own_columns)]
    unnamed x0 -> x3, local copies, waits for them, and re-layouts: none -> 1.24 us
    pallas_call x1, Pallas kernels: 43.6 us -> 42.9 us  [body(): pl.pallas_call(functools.partial(kernel, sizes), out_shape=jax.ShapeDtype...]
where the time goes in v10:
time: 45.3 us; the launch traced here: 44.8 us
  Pallas kernels  42.9 us (95%)
  local copies, waits for them, and re-layouts  1.24 us (3%)
  between operations  0.67 us (1%)
    pallas_call x1, Pallas kernels, body(): pl.pallas_call(functools.partial(kernel, sizes), out_shape=jax.ShapeDtype...  42.9 us
    unnamed x3, local copies, waits for them, and re-layouts  1.24 us

profile of v10, /device:TPU:8, one launch (start us, length us, event | category | flops | bytes accessed | tf_op | source)
XLA Modules:
  0.0 44.8 jit_solution(5355937684478694792)
XLA Ops:
  0.7 0.0 copy-start
  0.7 0.6 %copy-done = s32[1,96]{1,0:T(1,128)S(1)} copy-done((s32[1,96]{1,0:T(1,128)S(1)}, s32[1,96]{1,0:T(1,128)}, u32[]{:S(2)}) %copy-start) | copy-done | bytes 408
  1.3 42.9 %shard_map.64 = bf16[16,128]{1,0:T(8,128)(2,1)S(1)} custom-call(bf16[1,2,4,576]{3,2,1,0:T(4,128)(2,1)} %q_hbm.1, bf16[6144,576]{1,0:T(8,128)(2,1)} %bitcast.4, s32[1,96]{1,0:T(1,128)S(1)} %copy-done, s32[1]{0:T(128)S(6)} %copy.8.length_hbm, bf16[4,512,128]{2,1,0:T(8,128)(2,1)} %up_hbm.1, bf16[512,896]{1,0:T(8,128)(2,1)} %out_hbm.1), custom_call_target="tpu_custom_call" | custom-call | tf_op jit(solution)/shard_map/pallas_call | solution.py:455
  44.2 0.6 %copy.9 = bf16[8,2,28]{2,1,0:T(2,128)(2,1)} copy(bf16[8,2,28]{2,1,0:T(2,128)(2,1)S(1)} %bitcast.3) | data formatting | bytes 1792
Async XLA Ops:
  0.7 0.7 %copy-start = (s32[1,96]{1,0:T(1,128)S(1)}, s32[1,96]{1,0:T(1,128)}, u32[]{:S(2)}) copy-start(s32[1,96]{1,0:T(1,128)} %page_hbm.1) | copy-start | bytes 1156

commit v11 on v10

--- a/solution.py
+++ b/solution.py
@@ -44,7 +44,6 @@
     w_placed,
     tails,
     scores,
-    probs,
     tops,
     numer,
     num_send,
@@ -220,12 +219,14 @@
             for low in range(n * tile_keys, (n + 1) * tile_keys, 128):
                 p = jnp.exp2((scores[c % 2, :, low : low + 128] - tops[c]).astype(BF16))
                 total = total + p.astype(F32)
-                probs[:, c * step_keys + low : c * step_keys + low + 128] = p
                 pieces.append(p)
         if found:
             largest = functools.reduce(jnp.maximum, found)
-        part = dot(jnp.concatenate(pieces, axis=1), keys[pl.ds(c * step_keys, step_keys), 0:half])
-        numer[0] = part if c == 0 else numer[0] * columns(shrink, half) + part
+        here = pl.ds(c * step_keys, step_keys)
+        part = dot(jnp.concatenate(pieces, axis=1), keys[here, 0:latent])
+        for h in range(2):
+            own = part[:, h * half : (h + 1) * half]
+            numer[h] = own if c == 0 else numer[h] * columns(shrink, half) + own
 
     top_column = tops[steps - 1]
     sum_column = jnp.broadcast_to(jnp.sum(total, axis=1, keepdims=True), (rows, 128))
@@ -252,13 +253,6 @@
             )
 
     send_half(0)
-
-    for c in range(steps):
-        here = pl.ds(c * step_keys, step_keys)
-        part = dot(probs[:, here], keys[here, half:latent])
-        if c + 1 < steps:
-            part = part * columns(jnp.exp2(tops[c] - tops[steps - 1]), half)
-        numer[1] = part if c == 0 else numer[1] + part
 
     send_half(1)
     done(q_all.at[pl.ds(block, rows - block)], qx_send)
@@ -419,7 +413,6 @@
         pltpu.VMEM((w_out.shape[0], NX * x_lanes), BF16),
         pltpu.VMEM((key_rows, 128), BF16),
         pltpu.VMEM((2, rows, step_keys), F32),
-        pltpu.VMEM((rows, key_rows), BF16),
         pltpu.VMEM((key_rows // step_keys, rows, 128), F32),
         pltpu.VMEM((2, rows, half), F32),
         pltpu.VMEM((2, rows, half), BF16),

time: 45.3 us -> 45.5 us (level)
  no operation moved by 1% of the time
where the time goes in v11:
time: 45.5 us; the launch traced here: 45 us
  Pallas kernels  43.1 us (95%)
  local copies, waits for them, and re-layouts  1.24 us (3%)
  between operations  0.67 us (1%)
    pallas_call x1, Pallas kernels, body(): pl.pallas_call(functools.partial(kernel, sizes), out_shape=jax.ShapeDtype...  43.1 us
    unnamed x3, local copies, waits for them, and re-layouts  1.24 us

profile of v11, /device:TPU:8, one launch (start us, length us, event | category | flops | bytes accessed | tf_op | source)
XLA Modules:
  0.0 45.0 jit_solution(14128456539666920083)
XLA Ops:
  0.7 0.0 copy-start
  0.7 0.6 %copy-done = s32[1,96]{1,0:T(1,128)S(1)} copy-done((s32[1,96]{1,0:T(1,128)S(1)}, s32[1,96]{1,0:T(1,128)}, u32[]{:S(2)}) %copy-start) | copy-done | bytes 408
  1.3 43.1 %shard_map.64 = bf16[16,128]{1,0:T(8,128)(2,1)S(1)} custom-call(bf16[1,2,4,576]{3,2,1,0:T(4,128)(2,1)} %q_hbm.1, bf16[6144,576]{1,0:T(8,128)(2,1)} %bitcast.4, s32[1,96]{1,0:T(1,128)S(1)} %copy-done, s32[1]{0:T(128)S(6)} %copy.8.length_hbm, bf16[4,512,128]{2,1,0:T(8,128)(2,1)} %up_hbm.1, bf16[512,896]{1,0:T(8,128)(2,1)} %out_hbm.1), custom_call_target="tpu_custom_call" | custom-call | tf_op jit(solution)/shard_map/pallas_call | solution.py:448
  44.4 0.6 %copy.9 = bf16[8,2,28]{2,1,0:T(2,128)(2,1)} copy(bf16[8,2,28]{2,1,0:T(2,128)(2,1)S(1)} %bitcast.3) | data formatting | bytes 1792
Async XLA Ops:
  0.7 0.7 %copy-start = (s32[1,96]{1,0:T(1,128)S(1)}, s32[1,96]{1,0:T(1,128)}, u32[]{:S(2)}) copy-start(s32[1,96]{1,0:T(1,128)} %page_hbm.1) | copy-start | bytes 1156

commit v12 on v11

--- a/solution.py
+++ b/solution.py
@@ -228,6 +228,18 @@
             own = part[:, h * half : (h + 1) * half]
             numer[h] = own if c == 0 else numer[h] * columns(shrink, half) + own
 
+    def send_half(h):
+        num_send[h] = numer[h].astype(BF16)
+        for k in far_x:
+            send(
+                num_send.at[h, pl.ds(k * block, block)],
+                num_recv.at[h, k],
+                nx_send.at[h],
+                nx_recv.at[h],
+                along_x(-k),
+            )
+
+    send_half(0)
     top_column = tops[steps - 1]
     sum_column = jnp.broadcast_to(jnp.sum(total, axis=1, keepdims=True), (rows, 128))
     owner = lax.div(lax.broadcasted_iota(jnp.int32, (8, 128), 1), 8)
@@ -241,18 +253,6 @@
     for k in far_x:
         send(stat_send.at[k], stat_recv.at[k], st_send, st_recv, along_x(-k))
 
-    def send_half(h):
-        num_send[h] = numer[h].astype(BF16)
-        for k in far_x:
-            send(
-                num_send.at[h, pl.ds(k * block, block)],
-                num_recv.at[h, k],
-                nx_send.at[h],
-                nx_recv.at[h],
-                along_x(-k),
-            )
-
-    send_half(0)
 
     send_half(1)
     done(q_all.at[pl.ds(block, rows - block)], qx_send)

time: 45.5 us -> 45.8 us (level)
  no operation moved by 1% of the time
where the time goes in v12:
time: 45.8 us; the launch traced here: 45.5 us
  Pallas kernels  43.5 us (95%)
  local copies, waits for them, and re-layouts  1.24 us (3%)
  between operations  0.67 us (1%)
    pallas_call x1, Pallas kernels, body(): pl.pallas_call(functools.partial(kernel, sizes), out_shape=jax.ShapeDtype...  43.5 us
    unnamed x3, local copies, waits for them, and re-layouts  1.24 us

profile of v12, /device:TPU:8, one launch (start us, length us, event | category | flops | bytes accessed | tf_op | source)
XLA Modules:
  0.0 45.5 jit_solution(9094559620744653883)
XLA Ops:
  0.7 0.0 copy-start
  0.7 0.6 %copy-done = s32[1,96]{1,0:T(1,128)S(1)} copy-done((s32[1,96]{1,0:T(1,128)S(1)}, s32[1,96]{1,0:T(1,128)}, u32[]{:S(2)}) %copy-start) | copy-done | bytes 408
  1.3 43.5 %shard_map.64 = bf16[16,128]{1,0:T(8,128)(2,1)S(1)} custom-call(bf16[1,2,4,576]{3,2,1,0:T(4,128)(2,1)} %q_hbm.1, bf16[6144,576]{1,0:T(8,128)(2,1)} %bitcast.4, s32[1,96]{1,0:T(1,128)S(1)} %copy-done, s32[1]{0:T(128)S(6)} %copy.8.length_hbm, bf16[4,512,128]{2,1,0:T(8,128)(2,1)} %up_hbm.1, bf16[512,896]{1,0:T(8,128)(2,1)} %out_hbm.1), custom_call_target="tpu_custom_call" | custom-call | tf_op jit(solution)/shard_map/pallas_call | solution.py:448
  44.9 0.6 %copy.9 = bf16[8,2,28]{2,1,0:T(2,128)(2,1)} copy(bf16[8,2,28]{2,1,0:T(2,128)(2,1)S(1)} %bitcast.3) | data formatting | bytes 1792
Async XLA Ops:
  0.7 0.7 %copy-start = (s32[1,96]{1,0:T(1,128)S(1)}, s32[1,96]{1,0:T(1,128)}, u32[]{:S(2)}) copy-start(s32[1,96]{1,0:T(1,128)} %page_hbm.1) | copy-start | bytes 1156
